TPU v7x, 256 devices: a whole 4x4x8 slice. The times are simulated.
256 devices in a mesh: slab: 256 (over x, z, y, core).
Axes of the slice: x: 4, y: 4, z: 8, core: 2. Of those that a mesh axis runs over, the one named last changes fastest.
Arguments:
- velocity: bfloat16 [3, 1024, 16, 4096], P(None, 'slab'), may hold values from -6 to 6
Outputs:
- composite: float32 [4, 32768], P(None, 'slab')
All inputs are finite; a program needn't handle non-finite values.
Results may differ from a plain program's by a relative error of at most 0.00085.
Values may be sent and summed in bfloat16 or wider, within the bound.
No kernel may reach another device: no remote copies, remote signals or barrier semaphores. Data moves between devices by JAX's collectives and lax.ppermute only.
A program may use at most 192 MiB of HBM per device.

v0:
```python
import jax
import jax.numpy as jnp
from jax import lax
from jax.sharding import PartitionSpec as P

taps = (1.0 / 16.0, 4.0 / 16.0, 6.0 / 16.0, 4.0 / 16.0, 1.0 / 16.0)
opacity_gain = 5.0
colour_gain = 2.0


def with_halo(array, sides, width):
    for axis, dim in sides:
        devices, length = (lax.axis_size(axis), array.shape[dim])
        up = [(i, (i + 1) % devices) for i in range(devices)]
        down = [(j, i) for i, j in up]
        last = lax.slice_in_dim(array, length - width, length, axis=dim)
        first = lax.slice_in_dim(array, 0, width, axis=dim)
        before = lax.ppermute(last, axis, up)
        after = lax.ppermute(first, axis, down)
        array = jnp.concatenate([before, array, after], axis=dim)
    return array


def entering(array, axis, join, neutral):
    place = lax.axis_index(axis)
    gathered = lax.all_gather(array.astype(jnp.bfloat16), axis)
    state = jnp.zeros_like(array) + jnp.asarray(neutral, array.dtype)

    def one(hop, state):
        return join(state, lax.dynamic_index_in_dim(gathered, hop, 0, False).astype(array.dtype))

    return lax.fori_loop(0, place, one, state)


def smooth_valid(field, along):
    length = field.shape[along]
    total = taps[0] * lax.slice_in_dim(field, 0, length - 4, axis=along)
    for offset in range(1, 5):
        total = total + taps[offset] * lax.slice_in_dim(
            field, offset, length - 4 + offset, axis=along
        )
    return total


def smooth_wrap(field, along):
    total = taps[0] * jnp.roll(field, 2, along)
    for offset in range(1, 5):
        total = total + taps[offset] * jnp.roll(field, 2 - offset, along)
    return total


def derive_valid(field, along):
    length = field.shape[along]
    first = lax.slice_in_dim(field, 0, length - 4, axis=along)
    second = lax.slice_in_dim(field, 1, length - 3, axis=along)
    fourth = lax.slice_in_dim(field, 3, length - 1, axis=along)
    fifth = lax.slice_in_dim(field, 4, length, axis=along)
    return (first - 8.0 * second + 8.0 * fourth - fifth) / 12.0


def derive_wrap(field, along):
    return (
        jnp.roll(field, 2, along)
        - 8.0 * jnp.roll(field, 1, along)
        + 8.0 * jnp.roll(field, -1, along)
        - jnp.roll(field, -2, along)
    ) / 12.0


def slab_image(smoothed, planes_total):
    comp_x = smoothed[0]
    comp_y = smoothed[1]
    comp_z = smoothed[2]

    def along_z(field):
        return derive_valid(field, 0)[:, 2:-2]

    def along_y(field):
        return derive_valid(field[2:-2], 1)

    def along_x(field):
        return derive_wrap(field[2:-2, 2:-2], 2)

    curl_x = along_y(comp_z) - along_z(comp_y)
    curl_y = along_z(comp_x) - along_x(comp_z)
    curl_z = along_x(comp_y) - along_y(comp_x)
    density = opacity_gain * (curl_x * curl_x + curl_y * curl_y + curl_z * curl_z) / planes_total
    colour = jax.nn.sigmoid(colour_gain * smoothed[:, 2:-2, 2:-2])
    running = jnp.cumsum(density, axis=0)
    before = jnp.concatenate([jnp.zeros_like(density[:1]), running[:-1]], axis=0)
    weight = jnp.exp(-before) * (1.0 - jnp.exp(-density))
    colour_sum = jnp.sum(weight[None] * colour, axis=1)
    colour_sum = colour_sum.reshape(3, -1)
    depth = jnp.sum(density, axis=0).reshape(-1)
    return (colour_sum, depth)


def add_depths(earlier, later):
    return earlier + later


def per_device(velocity):
    slab_count = lax.axis_size("slab")
    planes = velocity.shape[1]
    planes_total = planes * slab_count
    widened = with_halo(velocity, (("slab", 1),), 2)
    inner = smooth_wrap(smooth_valid(smooth_valid(widened.astype(jnp.float32), 1), 2), 3)
    smoothed = with_halo(inner.astype(jnp.bfloat16), (("slab", 1),), 2).astype(inner.dtype)
    colour_sum, depth = slab_image(smoothed, planes_total)
    nearer = entering(depth, "slab", add_depths, jnp.zeros_like(depth))
    through = jnp.exp(-nearer)
    terms = jnp.concatenate(
        [colour_sum * through[None], (through * (1.0 - jnp.exp(-depth)))[None]], axis=0
    )
    return lax.psum_scatter(terms, "slab", scatter_dimension=1, tiled=True)


def solution(mesh):
    in_specs = (P(None, "slab", None, None),)
    out_specs = P(None, "slab")
    return jax.shard_map(
        per_device, mesh=mesh, in_specs=in_specs, out_specs=out_specs, check_vma=False
    )
```

profile of v0, /device:TPU:1, one launch (start us, length us, event | category | flops | bytes accessed | tf_op | source)
XLA Modules:
  0.0 1851.3 jit_solution(1659242831625528149)
XLA Ops:
  6.5 0.0 copy-start.1
  6.5 0.0 all-gather.3.cloned.1.call-start
  6.5 1.6 fusion.62
  8.1 2.8 collective-permute-start
  10.9 0.6 collective-permute-start.1
  11.5 8.3 collective-permute-done
  19.8 2.8 collective-permute-done.1
  22.6 0.0 copy-done.1
  22.6 0.5 maximum_convert_fusion
  23.1 1.4 fusion.4
  24.5 1.8 fusion
  26.2 1.2 fusion.49
  27.4 1.2 fusion.51
  28.6 0.1 fusion.50
  28.7 0.1 fusion.52
  28.7 3.7 fusion.12
  32.4 0.1 fusion.61
  32.6 0.1 collective-permute-start.2
  32.7 7.0 collective-permute-start.3
  39.7 1.9 collective-permute-done.2
  41.6 2.7 collective-permute-done.3
  44.4 0.6 maximum_convert_fusion.1
  45.0 0.0 copy-start
  45.0 0.3 slice_bitcast_fusion.1
  45.3 0.4 fusion.56
  45.7 0.1 fusion.55
  45.8 0.4 fusion.54
  46.2 0.1 fusion.53
  46.2 1.4 copy-done
  47.6 0.5 slice_bitcast_fusion.3
  48.1 1.0 fusion.47
  49.2 0.8 reshape.53
  50.0 0.0 all-gather.3.cloned.1.call-update
  50.0 0.0 reduce-scatter.4.cloned.1.call-start
  50.1 3.1 fusion.64
  53.2 0.1 subtract_multiply_fusion
  53.4 2.4 fusion.18
  55.8 0.3 copy.5
  56.1 156.2 %all-gather.3.cloned.1.call-done = bf16[256,1,32768]{2,1,0:T(2,128)(2,1)} async-done(((bf16[1,1,32768]{2,1,0:T(2,128)(2,1)}), bf16[256,1,32768]{2,1,0:T(2,128)(2,1)}) %all-gather.3.cloned.1.call-update) | async-done | bytes 16777232 | tf_op jit(solution)/shard_map/all_gather | solution.py:26
  212.3 29.6 %copy.8 = bf16[256,1,32768]{2,0,1:T(8,128)(2,1)} copy(bf16[256,1,32768]{2,1,0:T(2,128)(2,1)} %all-gather.3.cloned.1.call-done) | data formatting | bytes 33554432
  241.9 1.2 while.10
  241.9 1.1 dynamic-slice_convert_fusion.2
  243.1 0.1 broadcast_multiply_fusion
  243.3 0.2 pad_maximum_fusion
  243.5 8.6 copy.2
  252.1 0.0 reduce-scatter.4.cloned.1.call-update
  252.1 1590.9 %reduce-scatter.4.cloned.1.call-done = f32[128,4]{1,0:T(8,128)} async-done(((f32[32768,4]{1,0:T(8,128)}), f32[128,4]{1,0:T(8,128)}) %reduce-scatter.4.cloned.1.call-update) | async-done | bytes 2064
  1843.0 1.5 copy.3
  (6 shorter events, 0.1 us)
Async XLA Ops:
  6.5 16.1 copy-start.1
  6.5 205.8 %all-gather.3.cloned.1.call-start = ((), (), s32[]{:S(2)}) async-start(), calls=%async_computation.1 | async-start | bytes 33685504 | tf_op jit(solution)/shard_map/all_gather | solution.py:26
  8.1 11.7 collective-permute-start
  10.9 11.7 collective-permute-start.1
  32.6 9.0 collective-permute-start.2
  32.7 11.7 collective-permute-start.3
  45.0 2.6 copy-start
  50.0 1793.0 %reduce-scatter.4.cloned.1.call-start = ((), (), s32[]{:S(2)}) async-start(), calls=%async_computation.2 | async-start | bytes 16842752
Sparse Core Ops, SparseCore 0:
  50.1 162.1 all-gather.2
  252.3 1590.6 reduce-scatter.3
where the time goes:
time: 1870 us; the launch traced here: 1850 us
  waiting for transfers between devices  1760 us (94%)
  local copies, waits for them, and re-layouts  47.5 us (3%)
    unnamed x3, waiting for transfers between devices  1590 us
    all_gather x1, waiting for transfers between devices, entering(): gathered = lax.all_gather(array.astype(jnp.bfloat16), axis)  156 us
    unnamed x10, local copies, waits for them, and re-layouts  42.1 us
  transfers between devices with their start and end apart: 6, of which 6 were waited for; matrix products, arithmetic and copies ran while one was open for 0% of the time, Pallas kernels for 0%

commit v1 on v0

v1 whole, which is shorter than its diff:
```python
import numpy as np
import jax
import jax.numpy as jnp
from jax import lax
from jax.experimental import pallas as pl
from jax.experimental.pallas import tpu as pltpu
from jax.sharding import PartitionSpec as P

NX = 4096
TILES = NX // 128
S_INT = {-2: 1, -1: 4, 0: 6, 1: 4, 2: 1}
D_INT = {-2: 1, -1: -8, 1: 8, 2: -1}
DS_INT = {}
for i, a in S_INT.items():
    for j, b in D_INT.items():
        DS_INT[i + j] = DS_INT.get(i + j, 0) + a * b
UX, UY, UZ = 0, 1, 2
OPACITY_GAIN = 5.0


def own_row(c, z, y):
    return (c * 4 + z) * 16 + y


PARTS = ((UX, True, 12), (UZ, True, 12), (UY, True, 8), (UX, False, 8), (UY, False, 8))


def message_rows():
    rows = []
    for c, inner, count in PARTS:
        for k in range(2):
            for i in range(count):
                rows.append((c, inner, k, i + (2 if count == 12 else 4)))
    return rows


def message_plane(inner, k, up):
    return (2 + k if inner else k) if up else (k if inner else 2 + k)


def send_matrix(up):
    w = np.zeros((96, 192), np.float32)
    for n, (c, inner, k, y) in enumerate(message_rows()):
        for dy, t in S_INT.items():
            w[n, own_row(c, message_plane(inner, k, up), y + dy)] += t
    return w


TERMS = (
    (0, UX, "S", "S", 1),
    (1, UY, "S", "S", 1),
    (2, UZ, "S", "S", 1),
    (3, UZ, "S", "D", 1),
    (3, UY, "D", "S", -1),
    (4, UX, "D", "S", 1),
    (5, UX, "S", "D", -1),
)


def field_matrices():
    own = np.zeros((192, 192), np.float32)
    halo = {False: np.zeros((192, 96), np.float32), True: np.zeros((192, 96), np.float32)}
    place = {up: {} for up in (False, True)}
    for up in (False, True):
        for n, (c, inner, k, y) in enumerate(message_rows()):
            plane = message_plane(inner, k, up) + (-4 if up else 4)
            place[up][c, plane, y] = n
    along = {"S": S_INT, "D": DS_INT}
    for field, c, fz, fy, sign in TERMS:
        for p in range(4):
            for r in range(8):
                m = field * 32 + p * 8 + r
                for dz, a in along[fz].items():
                    q = p + dz
                    if 0 <= q < 4:
                        for dy, b in along[fy].items():
                            own[m, own_row(c, q, r + 4 + dy)] += sign * a * b
                    else:
                        up = q < 0
                        if fy == "S":
                            halo[up][m, place[up][c, q, r + 4]] += sign * a
                        else:
                            for dy, b in D_INT.items():
                                halo[up][m, place[up][c, q, r + 4 + dy]] += sign * a * b
    return own, halo[True], halo[False]


def matrices():
    up, down = send_matrix(True), send_matrix(False)
    send = np.stack([np.concatenate([down, up]), np.concatenate([up, down])])
    own, prev, nxt = field_matrices()
    field = np.stack([np.concatenate([own, prev, nxt], 1), np.concatenate([own, nxt, prev], 1)])
    return send.astype(jnp.bfloat16), field.astype(jnp.bfloat16)


def core_index():
    return lax.rem(lax.axis_index("slab"), 2)


def pack_kernel(w_ref, x_ref, a_ref, b_ref):
    w = w_ref[core_index()]
    out = jnp.dot(w, x_ref[...], preferred_element_type=jnp.float32).astype(jnp.bfloat16)
    a_ref[...] = out[:96]
    b_ref[...] = out[96:]


def pack(w, x):
    chunk = 1024
    return pl.pallas_call(
        pack_kernel,
        grid=(NX // chunk,),
        out_shape=[jax.ShapeDtypeStruct((96, NX), jnp.bfloat16)] * 2,
        in_specs=[
            pl.BlockSpec((2, 192, 192), lambda i: (0, 0, 0)),
            pl.BlockSpec((192, chunk), lambda i: (0, i)),
        ],
        out_specs=[pl.BlockSpec((96, chunk), lambda i: (0, i))] * 2,
        compiler_params=pltpu.CompilerParams(vmem_limit_bytes=32 << 20),
        name="pack_halo",
    )(w, x)


def slab_kernel(w_ref, x_ref, a_ref, b_ref, keep_ref, send_ref, field_ref):
    core = core_index()
    w = w_ref[core]
    chunk = 512

    def multiply(n, carry):
        cols = pl.ds(pl.multiple_of(n * chunk, chunk), chunk)
        rows = jnp.concatenate([x_ref[:, cols], a_ref[:, cols], b_ref[:, cols]], axis=0)
        field_ref[:, cols] = jnp.dot(w, rows, preferred_element_type=jnp.float32)
        return carry

    lax.fori_loop(0, NX // chunk, multiply, 0)
    lane = lax.broadcasted_iota(jnp.int32, (32, 128), 1)

    def tile(t, out_ref, row):
        def cols(k):
            return pl.ds(pl.multiple_of(lax.rem(t + k + TILES, TILES) * 128, 128), 128)

        at = [cols(-1), cols(0), cols(1)]

        def load(field):
            return [field_ref[field * 32 : field * 32 + 32, at[k]] for k in range(3)]

        def ahead(v, i):
            return pltpu.roll(jnp.where(lane < i, v[2], v[1]), 128 - i, 1)

        def behind(v, i):
            return pltpu.roll(jnp.where(lane >= 128 - i, v[0], v[1]), i, 1)

        def smooth(v, a1, b1, a2, b2):
            return 6.0 * v[1] + 4.0 * (a1 + b1) + (a2 + b2)

        def smoothed(field):
            v = load(field)
            return smooth(v, ahead(v, 1), behind(v, 1), ahead(v, 2), behind(v, 2))

        def smoothed_and_derivative(field):
            v = load(field)
            ups = [ahead(v, i) for i in range(1, 5)]
            downs = [behind(v, i) for i in range(1, 5)]
            difference = [u - d for u, d in zip(ups, downs)]
            derivative = 36.0 * difference[0] + 26.0 * difference[1] + (4.0 * difference[2] - difference[3])
            return smooth(v, ups[0], downs[0], ups[1], downs[1]), derivative

        s_x = smoothed(0)
        s_y, dx_y = smoothed_and_derivative(1)
        s_z, dx_z = smoothed_and_derivative(2)
        curl_x = smoothed(3)
        curl_y = smoothed(4) - dx_z
        curl_z = smoothed(5) + dx_y
        density = (curl_x * curl_x + curl_y * curl_y + curl_z * curl_z) * (OPACITY_GAIN / 1024.0 / 49152.0**2)
        colours = [0.5 + 0.5 * jnp.tanh(s * (1.0 / 4096.0)) for s in (s_x, s_y, s_z)]
        opacity = 1.0 - jnp.exp(-density)
        depth = density[:8]
        weight = opacity[:8]
        sums = [weight * c[:8] for c in colours]
        for p in range(1, 4):
            part = slice(8 * p, 8 * p + 8)
            weight = jnp.exp(-depth) * opacity[part]
            sums = [s + weight * c[part] for s, c in zip(sums, colours)]
            depth = depth + density[part]
        for f, value in enumerate(sums + [depth]):
            out_ref[pl.ds(row * 4 + f, 8, stride=64), :] = value

    def pair(i, carry):
        tile(2 * i + core, keep_ref, i)
        tile(2 * i + 1 - core, send_ref, i)
        return carry

    lax.fori_loop(0, TILES // 2, pair, 0)


def slab_image(w, x, a, b):
    vmem = pl.BlockSpec(memory_space=pltpu.VMEM)
    return pl.pallas_call(
        slab_kernel,
        out_shape=[jax.ShapeDtypeStruct((512, 128), jnp.float32)] * 2,
        in_specs=[vmem] * 4,
        out_specs=[vmem] * 2,
        scratch_shapes=[pltpu.VMEM((192, NX), jnp.float32)],
        compiler_params=pltpu.CompilerParams(vmem_limit_bytes=32 << 20),
        name="slab_image",
    )(w, x, a, b)


def merge_kernel(own_ref, other_ref, out_ref):
    first = core_index() == 0

    def rows(f):
        return pl.ds(f, 128, stride=4)

    own_depth, other_depth = own_ref[rows(3), :], other_ref[rows(3), :]
    zero = jnp.zeros_like(own_depth)
    own_scale = jnp.exp(-jnp.where(first, zero, other_depth))
    other_scale = jnp.exp(-jnp.where(first, own_depth, zero))
    for f in range(3):
        out_ref[rows(f), :] = own_scale * own_ref[rows(f), :] + other_scale * other_ref[rows(f), :]
    out_ref[rows(3), :] = own_depth + other_depth


def merge(own, other):
    vmem = pl.BlockSpec(memory_space=pltpu.VMEM)
    return pl.pallas_call(
        merge_kernel,
        out_shape=jax.ShapeDtypeStruct((512, 128), jnp.float32),
        in_specs=[vmem] * 2,
        out_specs=vmem,
        compiler_params=pltpu.CompilerParams(vmem_limit_bytes=8 << 20),
        name="merge_cores",
    )(own, other)


def composite_kernel(in_ref, out_ref):
    def part(v, f):
        return in_ref[pl.ds(v * 4 + f, 8, stride=64), :]

    depth = part(0, 3)
    sums = [part(0, f) for f in range(3)]
    for v in range(1, 16):
        through = jnp.exp(-depth)
        sums = [s + through * part(v, f) for f, s in enumerate(sums)]
        depth = depth + part(v, 3)
    nearer = [jnp.zeros((1, 128), jnp.float32)]
    for s in range(8):
        nearer.append(nearer[-1] + depth[s : s + 1])
    through = jnp.exp(-jnp.concatenate(nearer[:8], axis=0))
    for f in range(3):
        out_ref[f : f + 1, :] = jnp.sum(through * sums[f], axis=0, keepdims=True)
    out_ref[3:4, :] = 1.0 - jnp.exp(-nearer[8])


def composite(parts):
    vmem = pl.BlockSpec(memory_space=pltpu.VMEM)
    return pl.pallas_call(
        composite_kernel,
        out_shape=jax.ShapeDtypeStruct((4, 128), jnp.float32),
        in_specs=[vmem],
        out_specs=vmem,
        compiler_params=pltpu.CompilerParams(vmem_limit_bytes=8 << 20),
        name="composite_chips",
    )(parts)


def solution(mesh):
    devices = mesh.shape["slab"]
    send_weights, field_weights = matrices()
    across = [(i, (i + 1) % devices if i % 2 else (i - 1) % devices) for i in range(devices)]
    within = [(i, i ^ 1) for i in range(devices)]
    same_core = [list(range(k, devices, 2)) for k in range(2)]

    def per_device(velocity):
        x = velocity.reshape(192, NX)
        to_chip, to_core = pack(jnp.asarray(send_weights), x)
        from_chip = lax.ppermute(to_chip, "slab", across)
        from_core = lax.ppermute(to_core, "slab", within)
        keep, send = slab_image(jnp.asarray(field_weights), x, from_chip, from_core)
        other = lax.ppermute(send, "slab", within)
        merged = merge(keep, other).reshape(128, 4, 128)
        gathered = lax.all_to_all(merged, "slab", 0, 0, axis_index_groups=same_core, tiled=True)
        return composite(gathered.reshape(512, 128))

    return jax.shard_map(per_device, mesh=mesh, in_specs=(P(None, "slab", None, None),), out_specs=P(None, "slab"), check_vma=False)
```

time: 1870 us -> 59.8 us (0.03)
  waiting for transfers between devices: 1760 us -> 3.07 us
  local copies, waits for them, and re-layouts: 47.5 us -> 3.3 us
  blocking collectives: 0 us -> 23.7 us
    unnamed x3 -> x0, waiting for transfers between devices: 1590 us -> none
    all_gather x1 -> x0, waiting for transfers between devices: 156 us -> none  [entering(): gathered = lax.all_gather(array.astype(jnp.bfloat16), axis)]
    unnamed x10 -> x8, local copies, waits for them, and re-layouts: 42.1 us -> 3.3 us
    all_to_all x0 -> x1, blocking collectives: none -> 23.7 us  [per_device(): lax.all_to_all(merged, 'slab', 0, 0, axis_index_groups=same_core, tiled=T...]
  transfers between devices with their start and end apart: 6 -> 3, of which waited for: 6 -> 3; matrix products, arithmetic and copies ran while one was open for 0% -> 0% of each run, Pallas kernels for 0% -> 0%
where the time goes in v1:
time: 59.8 us; the launch traced here: 59.6 us
  blocking collectives  23.7 us (40%)
  starting transfers between devices  19.4 us (32%)
  Pallas kernels  10.2 us (17%)
  local copies, waits for them, and re-layouts  3.3 us (6%)
  waiting for transfers between devices  3.07 us (5%)
    all_to_all x1, blocking collectives, per_device(): lax.all_to_all(merged, 'slab', 0, 0, axis_index_groups=same_core, tiled=T...  23.7 us
    ppermute x1, starting transfers between devices, per_device(): from_core = lax.ppermute(to_core, 'slab', within)  8.76 us
    pallas_call x1, Pallas kernels, slab_image(): pl.pallas_call(slab_kernel, out_shape=[jax.ShapeDtypeStruct((512, 128), j...  8.1 us
    ppermute x1, starting transfers between devices, per_device(): other = lax.ppermute(send, 'slab', within)  7.85 us
    unnamed x8, local copies, waits for them, and re-layouts  3.3 us
    ppermute x1, starting transfers between devices, per_device(): from_chip = lax.ppermute(to_chip, 'slab', across)  2.78 us
    pallas_call x1, Pallas kernels, pack(): pl.pallas_call(pack_kernel, grid=(NX // chunk,), out_shape=[jax.ShapeDtyp...  1.27 us
    ppermute x1, waiting for transfers between devices, per_device(): from_chip = lax.ppermute(to_chip, 'slab', across)  1.21 us
  transfers between devices with their start and end apart: 3, of which 3 were waited for; matrix products, arithmetic and copies ran while one was open for 0% of the time, Pallas kernels for 0%

profile of v1, /device:TPU:1, one launch (start us, length us, event | category | flops | bytes accessed | tf_op | source)
XLA Modules:
  0.0 59.6 jit_solution(3968137254559471727)
XLA Ops:
  0.0 0.0 copy-start
  0.0 1.4 %copy-done = bf16[3,4,16,4096]{3,2,1,0:T(8,128)(2,1)S(1)} copy-done((bf16[3,4,16,4096]{3,2,1,0:T(8,128)(2,1)S(1)}, bf16[3,4,16,4096]{3,2,1,0:T(8,128)(2,1)}, u32[]{:S(2)}) %copy-start) | copy-done | bytes 1572888
  1.4 0.0 copy-start.3
  1.4 0.9 %copy-done.3 = bf16[2,192,192]{2,1,0:T(8,128)(2,1)S(1)} copy-done((bf16[2,192,192]{2,1,0:T(8,128)(2,1)S(1)}, bf16[2,192,192]{2,1,0:T(8,128)(2,1)}, u32[]{:S(2)}) %copy-start.3) | copy-done | bytes 147480
  2.3 0.0 copy-start.1
  2.3 1.3 %pack_halo.1 = (bf16[96,4096]{1,0:T(8,128)(2,1)S(1)}, bf16[96,4096]{1,0:T(8,128)(2,1)S(1)}) custom-call(bf16[2,192,192]{2,1,0:T(8,128)(2,1)S(1)} %copy-done.3, bf16[192,4096]{1,0:T(8,128)(2,1)S(1)} %bitcast.3), custom_call_target="tpu_custom_call" | custom-call | tf_op jit(solution)/shard_map/pack_halo/pallas_call | solution.py:109
  3.6 2.8 %collective-permute-start = (bf16[96,4096]{1,0:T(8,128)(2,1)S(1)}, bf16[96,4096]{1,0:T(8,128)(2,1)S(1)}, u32[]{:S(2)}, u32[]{:S(2)}) collective-permute-start(bf16[96,4096]{1,0:T(8,128)(2,1)S(1)} %get-tuple-element.9), channel_id=1, source_target_pairs={{0,255},{1,2},{2,1},{3,4},{4,3},{5,6},{6,5},{7,8},{8,7},{9,10},{10... | collective-permute-start | bytes 2359304 | tf_op jit(solution)/shard_map/ppermute | solution.py:276
  6.4 8.8 %collective-permute-start.1 = (bf16[96,4096]{1,0:T(8,128)(2,1)S(1)}, bf16[96,4096]{1,0:T(8,128)(2,1)S(1)}, u32[]{:S(2)}, u32[]{:S(2)}) collective-permute-start(bf16[96,4096]{1,0:T(8,128)(2,1)S(1)} %get-tuple-element.10), channel_id=1, source_target_pairs={{0,1},{1,0},{2,3},{3,2},{4,5},{5,4},{6,7},{7,6},{8,9},{9,8},{10,11... | collective-permute-start | bytes 2359304 | tf_op jit(solution)/shard_map/ppermute | solution.py:277
  15.2 1.2 %collective-permute-done.a_ref = bf16[96,4096]{1,0:T(8,128)(2,1)S(1)} collective-permute-done((bf16[96,4096]{1,0:T(8,128)(2,1)S(1)}, bf16[96,4096]{1,0:T(8,128)(2,1)S(1)}, u32[]{:S(2)}, u32[]{:S(2)}) %collective-permute-start) | collective-permute-done | bytes 786464 | tf_op jit(solution)/shard_map/ppermute | solution.py:276
  16.4 0.7 %collective-permute-done.1.b_ref = bf16[96,4096]{1,0:T(8,128)(2,1)S(1)} collective-permute-done((bf16[96,4096]{1,0:T(8,128)(2,1)S(1)}, bf16[96,4096]{1,0:T(8,128)(2,1)S(1)}, u32[]{:S(2)}, u32[]{:S(2)}) %collective-permute-start.1) | collective-permute-done | bytes 786464 | tf_op jit(solution)/shard_map/ppermute | solution.py:277
  17.1 0.0 copy-done.1
  17.1 0.0 copy-start.2
  17.1 1.0 %copy-done.2 = bf16[2,192,384]{2,1,0:T(8,128)(2,1)S(1)} copy-done((bf16[2,192,384]{2,1,0:T(8,128)(2,1)S(1)}, bf16[2,192,384]{2,1,0:T(8,128)(2,1)}, u32[]{:S(2)}) %copy-start.2) | copy-done | bytes 294936
  18.0 8.1 %slab_image.1 = (f32[512,128]{1,0:T(8,128)S(1)}, f32[512,128]{1,0:T(8,128)S(1)}) custom-call(bf16[2,192,384]{2,1,0:T(8,128)(2,1)S(1)} %copy-done.2, bf16[192,4096]{1,0:T(8,128)(2,1)S(1)} %bitcast.4, bf16[96,4096]{1,0:T(8,128)(2,1)S(1)} %collective-permute-done.a_ref, bf16[96,4096]{1,0:T(8,128)(2,1)S(1)} %collective-permute-done.1.b_ref), custom_call_target="tpu_custom_call" | custom-call | tf_op jit(solution)/shard_map/slab_image/pallas_call | solution.py:197
  26.1 7.8 %collective-permute-start.2 = (f32[512,128]{1,0:T(8,128)S(1)}, f32[512,128]{1,0:T(8,128)S(1)}, u32[]{:S(2)}, u32[]{:S(2)}) collective-permute-start(f32[512,128]{1,0:T(8,128)S(1)} %get-tuple-element.12), channel_id=1, source_target_pairs={{0,1},{1,0},{2,3},{3,2},{4,5},{5,4},{6,7},{7,6},{8,9},{9,8},{10,11... | collective-permute-start | bytes 786440 | tf_op jit(solution)/shard_map/ppermute | solution.py:279
  34.0 1.2 %collective-permute-done.2.other_ref = f32[512,128]{1,0:T(8,128)S(1)} collective-permute-done((f32[512,128]{1,0:T(8,128)S(1)}, f32[512,128]{1,0:T(8,128)S(1)}, u32[]{:S(2)}, u32[]{:S(2)}) %collective-permute-start.2) | collective-permute-done | bytes 262176 | tf_op jit(solution)/shard_map/ppermute | solution.py:279
  35.1 0.1 merge_cores.1
  35.2 23.7 %all_to_all.5 = f32[128,4,128]{2,1,0:T(4,128)S(1)} all-to-all(f32[128,4,128]{2,1,0:T(4,128)S(1)} %bitcast.5), channel_id=1, replica_groups={{0,2,4,6,8,10,12,14,16,18,20,22,24,26,28,30,32,34,36,38,40,42,44,46,48,..., dimensions={0} | all-to-all | bytes 524288 | tf_op jit(solution)/shard_map/all_to_all | solution.py:281
  58.9 0.7 %composite_chips.1 = f32[4,128]{1,0:T(4,128)} custom-call(f32[512,128]{1,0:T(8,128)S(1)} %bitcast.6), custom_call_target="tpu_custom_call" | custom-call | tf_op jit(solution)/shard_map/composite_chips/pallas_call | solution.py:256
Async XLA Ops:
  0.0 1.4 %copy-start = (bf16[3,4,16,4096]{3,2,1,0:T(8,128)(2,1)S(1)}, bf16[3,4,16,4096]{3,2,1,0:T(8,128)(2,1)}, u32[]{:S(2)}) copy-start(bf16[3,4,16,4096]{3,2,1,0:T(8,128)(2,1)} %param.3) | copy-start | bytes 4718596
  1.4 0.9 %copy-start.3 = (bf16[2,192,192]{2,1,0:T(8,128)(2,1)S(1)}, bf16[2,192,192]{2,1,0:T(8,128)(2,1)}, u32[]{:S(2)}) copy-start(bf16[2,192,192]{2,1,0:T(8,128)(2,1)} %constant.4.clone.w_ref) | copy-start | bytes 442372
  2.3 14.7 %copy-start.1 = (bf16[3,4,16,4096]{3,2,1,0:T(8,128)(2,1)S(1)}, bf16[3,4,16,4096]{3,2,1,0:T(8,128)(2,1)}, u32[]{:S(2)}) copy-start(bf16[3,4,16,4096]{3,2,1,0:T(8,128)(2,1)} %param.3) | copy-start | bytes 4718596
  3.6 12.7 %collective-permute-start = (bf16[96,4096]{1,0:T(8,128)(2,1)S(1)}, bf16[96,4096]{1,0:T(8,128)(2,1)S(1)}, u32[]{:S(2)}, u32[]{:S(2)}) collective-permute-start(bf16[96,4096]{1,0:T(8,128)(2,1)S(1)} %get-tuple-element.9), channel_id=1, source_target_pairs={{0,255},{1,2},{2,1},{3,4},{4,3},{5,6},{6,5},{7,8},{8,7},{9,10},{10... | collective-permute-start | bytes 2359304 | tf_op jit(solution)/shard_map/ppermute | solution.py:276
  6.4 10.7 %collective-permute-start.1 = (bf16[96,4096]{1,0:T(8,128)(2,1)S(1)}, bf16[96,4096]{1,0:T(8,128)(2,1)S(1)}, u32[]{:S(2)}, u32[]{:S(2)}) collective-permute-start(bf16[96,4096]{1,0:T(8,128)(2,1)S(1)} %get-tuple-element.10), channel_id=1, source_target_pairs={{0,1},{1,0},{2,3},{3,2},{4,5},{5,4},{6,7},{7,6},{8,9},{9,8},{10,11... | collective-permute-start | bytes 2359304 | tf_op jit(solution)/shard_map/ppermute | solution.py:277
  17.1 1.0 %copy-start.2 = (bf16[2,192,384]{2,1,0:T(8,128)(2,1)S(1)}, bf16[2,192,384]{2,1,0:T(8,128)(2,1)}, u32[]{:S(2)}) copy-start(bf16[2,192,384]{2,1,0:T(8,128)(2,1)} %constant.5.clone.w_ref) | copy-start | bytes 884740
  26.1 9.0 %collective-permute-start.2 = (f32[512,128]{1,0:T(8,128)S(1)}, f32[512,128]{1,0:T(8,128)S(1)}, u32[]{:S(2)}, u32[]{:S(2)}) collective-permute-start(f32[512,128]{1,0:T(8,128)S(1)} %get-tuple-element.12), channel_id=1, source_target_pairs={{0,1},{1,0},{2,3},{3,2},{4,5},{5,4},{6,7},{7,6},{8,9},{9,8},{10,11... | collective-permute-start | bytes 786440 | tf_op jit(solution)/shard_map/ppermute | solution.py:279

commit v2 on v1

v2 whole, which is shorter than its diff:
```python
import functools

import numpy as np
import jax
import jax.numpy as jnp
from jax import lax
from jax.experimental import pallas as pl
from jax.experimental.pallas import tpu as pltpu
from jax.sharding import PartitionSpec as P

NX = 4096
TILES = NX // 128
S_INT = {-2: 1, -1: 4, 0: 6, 1: 4, 2: 1}
D_INT = {-2: 1, -1: -8, 1: 8, 2: -1}
DS_INT = {}
for i, a in S_INT.items():
    for j, b in D_INT.items():
        DS_INT[i + j] = DS_INT.get(i + j, 0) + a * b
UX, UY, UZ = 0, 1, 2
OPACITY_GAIN = 5.0


def own_row(c, z, y):
    return (c * 4 + z) * 16 + y


PARTS = ((UX, True, 12), (UX, False, 8), (UY, True, 8), (UY, False, 8), (UZ, True, 12))


def message_rows():
    rows = []
    for c, inner, count in PARTS:
        for k in range(2):
            for i in range(count):
                rows.append((c, inner, k, i + (2 if count == 12 else 4)))
    return rows


def message_plane(inner, k, up):
    return (2 + k if inner else k) if up else (k if inner else 2 + k)


def send_matrix(up):
    w = np.zeros((96, 192), np.float32)
    for n, (c, inner, k, y) in enumerate(message_rows()):
        for dy, t in S_INT.items():
            w[n, own_row(c, message_plane(inner, k, up), y + dy)] += t
    return w


TERMS = (
    (0, UY, "S", "S", 1),
    (1, UZ, "S", "S", 1),
    (2, UZ, "S", "D", 1),
    (2, UY, "D", "S", -1),
    (3, UX, "S", "S", 1),
    (4, UX, "D", "S", 1),
    (5, UX, "S", "D", -1),
)
OWN_YZ, OWN_X, HALO_YZ, HALO_X = slice(64, 192), slice(0, 64), slice(32, 96), slice(0, 48)


def field_matrices():
    own = np.zeros((192, 192), np.float32)
    halo = {False: np.zeros((192, 96), np.float32), True: np.zeros((192, 96), np.float32)}
    place = {up: {} for up in (False, True)}
    for up in (False, True):
        for n, (c, inner, k, y) in enumerate(message_rows()):
            plane = message_plane(inner, k, up) + (-4 if up else 4)
            place[up][c, plane, y] = n
    along = {"S": S_INT, "D": DS_INT}
    for field, c, fz, fy, sign in TERMS:
        for p in range(4):
            for r in range(8):
                m = field * 32 + p * 8 + r
                for dz, a in along[fz].items():
                    q = p + dz
                    if 0 <= q < 4:
                        for dy, b in along[fy].items():
                            own[m, own_row(c, q, r + 4 + dy)] += sign * a * b
                    else:
                        up = q < 0
                        if fy == "S":
                            halo[up][m, place[up][c, q, r + 4]] += sign * a
                        else:
                            for dy, b in D_INT.items():
                                halo[up][m, place[up][c, q, r + 4 + dy]] += sign * a * b
    return own, halo[True], halo[False]


def line_matrix():
    w = np.zeros((256, 256), np.float32)
    for column, taps in ((0, S_INT), (128, DS_INT)):
        for j in range(128):
            for d, t in taps.items():
                row = j + d if 0 <= j + d < 128 else 128 + (j + d) % 128
                w[row, column + j] += t
    return w


def matrices():
    up, down = send_matrix(True), send_matrix(False)
    send = np.stack([np.concatenate([down, up]), np.concatenate([up, down])])
    own, prev, nxt = field_matrices()
    field = np.zeros((2, 192, 256), np.float32)
    for core, halo in enumerate(([prev, nxt], [nxt, prev])):
        field[core, :96] = np.concatenate([own[:96, OWN_YZ], *(h[:96, HALO_YZ] for h in halo)], 1)
        field[core, 96:, :160] = np.concatenate([own[96:, OWN_X], *(h[96:, HALO_X] for h in halo)], 1)
        assert not own[:96, OWN_X].any() and not own[96:, OWN_YZ].any()
        assert not any(h[:96, :32].any() or h[96:, 48:].any() for h in halo)
    return [m.astype(jnp.bfloat16) for m in (send, field, line_matrix())]


SEGMENTS = ((tuple(range(32)), tuple(range(32))),)
TURN = 123
GROUP = 8
HBM = pl.BlockSpec(memory_space=pltpu.HBM)
VMEM = pl.BlockSpec(memory_space=pltpu.VMEM)


def in_hbm(x):
    return pltpu.with_memory_space_constraint(jnp.asarray(x), pltpu.HBM)


def core_index():
    return lax.rem(lax.axis_index("slab"), 2)


def runs(tiles):
    out = []
    for place, tile in enumerate(tiles):
        tile %= TILES
        if out and out[-1][0] + out[-1][2] == tile:
            out[-1][2] += 1
        else:
            out.append([tile, place, 1])
    return out


def pack_kernel(segments, w_ref, f_ref, l_ref, x_ref, *refs):
    count = len(segments)
    packed, (fv_ref, lv_ref) = [refs[3 * n : 3 * n + 3] for n in range(count)], refs[3 * count : 3 * count + 2]
    wv_ref, sems = refs[3 * count + 2 :]
    core = core_index()
    first = pltpu.make_async_copy(w_ref.at[core], wv_ref, sems.at[0])
    first.start()
    parts = []
    for tiles, (a_ref, b_ref, xv_ref) in zip(segments, packed):
        for tile, place, length in runs(tiles):
            for k in range(0, length, 16):
                n = min(16, length - k)
                cols = slice((place + k) * 128, (place + k + n) * 128)
                source = x_ref.at[:, pl.ds((tile + k) * 128, n * 128)]
                copy = pltpu.make_async_copy(source, xv_ref.at[:, cols], sems.at[len(parts) + 1])
                copy.start()
                parts.append((copy, a_ref, b_ref, xv_ref, cols))
    later = [
        pltpu.make_async_copy(f_ref.at[core], fv_ref, sems.at[len(parts) + 1]),
        pltpu.make_async_copy(l_ref, lv_ref, sems.at[len(parts) + 2]),
    ]
    for copy in later:
        copy.start()
    first.wait()
    for copy, a_ref, b_ref, xv_ref, cols in parts:
        copy.wait()
        out = jnp.dot(wv_ref[...], xv_ref[:, cols], preferred_element_type=jnp.float32).astype(jnp.bfloat16)
        a_ref[:, cols] = out[:96]
        b_ref[:, cols] = out[96:]
    for copy in later:
        copy.wait()


def pack(segments, w, field_w, line_w, x):
    out = []
    for tiles in segments:
        width = len(tiles) * 128
        out += [(96, width), (96, width), (192, width)]
    out += [(192, 256), (256, 256)]
    *packed, field_w, line_w = pl.pallas_call(
        functools.partial(pack_kernel, segments),
        out_shape=[jax.ShapeDtypeStruct(shape, jnp.bfloat16) for shape in out],
        in_specs=[HBM] * 4,
        out_specs=[VMEM] * len(out),
        scratch_shapes=[pltpu.VMEM((192, 192), jnp.bfloat16), pltpu.SemaphoreType.DMA((24,))],
        compiler_params=pltpu.CompilerParams(vmem_limit_bytes=16 << 20),
        name="pack_halo",
    )(w, field_w, line_w, x)
    return [packed[n : n + 3] for n in range(0, len(packed), 3)], field_w, line_w


def slab_kernel(tiles, image, before, after, *refs):
    w_ref, l_ref, x_ref, a_ref, b_ref = refs[:5]
    edges = dict(zip(before, refs[5:]))
    keep_ref, send_ref, *out_edges = refs[5 + len(before) :]
    core = core_index()
    half = lax.broadcasted_iota(jnp.int32, (192, 128), 1) < 64
    place = {tile % TILES: n for n, tile in enumerate(tiles)}
    fields = {}

    def field(t):
        t %= TILES
        if t in edges:
            return edges[t][:192, :], edges[t][192:, :]
        if t not in fields:
            n = place[t] // 2 * 2
            cols = slice(n * 128, min(n + 2, len(tiles)) * 128)
            yz = jnp.concatenate([x_ref[OWN_YZ, cols], a_ref[HALO_YZ, cols], b_ref[HALO_YZ, cols]], axis=0)
            x = jnp.concatenate([x_ref[OWN_X, cols], a_ref[HALO_X, cols], b_ref[HALO_X, cols]], axis=0)
            out = jnp.concatenate(
                [
                    jnp.dot(w_ref[:96, :], yz, preferred_element_type=jnp.float32),
                    jnp.dot(w_ref[96:, :160], x, preferred_element_type=jnp.float32),
                ],
                axis=0,
            )
            high = out.astype(jnp.bfloat16)
            low = (out - high.astype(jnp.float32)).astype(jnp.bfloat16)
            for k, tile in enumerate(tiles[n : n + 2]):
                part = slice(k * 128, k * 128 + 128)
                tile %= TILES
                fields[tile] = high[:, part], low[:, part]
                if tile in after:
                    ref = out_edges[after.index(tile)]
                    ref[:192, :], ref[192:, :] = fields[tile]
        return fields[t]

    def line(t):
        out = []
        for previous, here, following in zip(field(t - 1), field(t), field(t + 1)):
            out += [here, jnp.where(half, following, previous)]
        return jnp.concatenate(out, axis=1)

    def tile_group(group):
        lines = [line(t) for t in group]
        both = jnp.concatenate([l_ref[...]] * 2, axis=0)
        yz = jnp.dot(jnp.concatenate([v[:64] for v in lines], axis=0), both, preferred_element_type=jnp.float32)
        rest = jnp.dot(jnp.concatenate([v[64:] for v in lines], axis=0), both[:, :128], preferred_element_type=jnp.float32)
        return [tile(yz[n * 64 : n * 64 + 64], rest[n * 128 : n * 128 + 128]) for n in range(len(group))]

    def tile(yz, rest):
        smoothed = [rest[32:64], yz[:32, :128], yz[32:, :128]]
        curl = [rest[:32], rest[64:96] - yz[32:, 128:], rest[96:] + yz[:32, 128:]]
        density = (curl[0] * curl[0] + curl[1] * curl[1] + curl[2] * curl[2]) * (OPACITY_GAIN / 1024.0 / 49152.0**2)
        colours = [0.5 + 0.5 * jnp.tanh(s * (1.0 / 4096.0)) for s in smoothed]
        opacity = 1.0 - jnp.exp(-density)
        depth = density[:8]
        weight = opacity[:8]
        sums = [weight * c[:8] for c in colours]
        for p in range(1, 4):
            part = slice(8 * p, 8 * p + 8)
            weight = jnp.exp(-depth) * opacity[part]
            sums = [s + weight * c[part] for s, c in zip(sums, colours)]
            depth = depth + density[part]
        return sums + [depth]

    pairs = len(image) // 2
    for first in range(0, len(image), GROUP):
        values = tile_group(image[first : first + GROUP])
        for n in range(0, len(values), 2):
            for f, (a, b) in enumerate(zip(values[n], values[n + 1])):
                row = (f * pairs + (first + n) // 2) * 8
                keep_ref[row : row + 8, :] = jnp.where(core == 0, a, b)
                send_ref[row : row + 8, :] = jnp.where(core == 0, b, a)


def slab_image(tiles, image, before, after, *arrays):
    pairs = len(image) // 2
    out = [jax.ShapeDtypeStruct((pairs * 32, 128), jnp.float32)] * 2 + [jax.ShapeDtypeStruct((384, 128), jnp.bfloat16)] * len(after)
    return pl.pallas_call(
        functools.partial(slab_kernel, tiles, image, before, after),
        out_shape=out,
        in_specs=[VMEM] * len(arrays),
        out_specs=[VMEM] * len(out),
        compiler_params=pltpu.CompilerParams(vmem_limit_bytes=16 << 20),
        cost_estimate=pl.CostEstimate(flops=2 * 192 * 1024 * 128 * len(tiles), bytes_accessed=1 << 20, transcendentals=0),
        name="slab_image",
    )(*arrays)


def merge_kernel(images, *refs):
    first = core_index() == 0
    out_ref = refs[-1]
    for image, own_ref, other_ref in zip(images, refs[0:-1:2], refs[1:-1:2]):
        pairs = len(image) // 2
        own, other = ([ref[f * pairs * 8 : (f + 1) * pairs * 8, :] for f in range(4)] for ref in (own_ref, other_ref))
        zero = jnp.zeros_like(own[3])
        own_scale = jnp.exp(-jnp.where(first, zero, other[3]))
        other_scale = jnp.exp(-jnp.where(first, own[3], zero))
        merged = [own_scale * a + other_scale * b for a, b in zip(own[:3], other[:3])] + [own[3] + other[3]]
        for f in range(4):
            for n in range(pairs):
                rank = ((image[0] // 2 + n) % (TILES // 2) - TURN) % 128
                value, turn = merged[f][n * 8 : n * 8 + 8], rank // 16
                out_ref[pl.ds(rank % 16 * 4 + f, 8, stride=64), :] = pltpu.roll(value, turn, 0) if turn else value


def merge(images, arrays):
    return pl.pallas_call(
        functools.partial(merge_kernel, images),
        out_shape=jax.ShapeDtypeStruct((512, 128), jnp.float32),
        in_specs=[VMEM] * len(arrays),
        out_specs=VMEM,
        compiler_params=pltpu.CompilerParams(vmem_limit_bytes=8 << 20),
        name="merge_cores",
    )(*arrays)


def composite_kernel(in_ref, out_ref):
    lead = (-TURN) % 128 // 16

    def part(v, f):
        rank = (v - TURN) % 128
        value = in_ref[pl.ds(rank % 16 * 4 + f, 8, stride=64), :]
        turn = (lead - rank // 16) % 8
        return pltpu.roll(value, turn, 0) if turn else value

    depth = part(0, 3)
    sums = [part(0, f) for f in range(3)]
    for v in range(1, 16):
        through = jnp.exp(-depth)
        sums = [s + through * part(v, f) for f, s in enumerate(sums)]
        depth = depth + part(v, 3)
    nearer, total = {}, jnp.zeros((1, 128), jnp.float32)
    for segment in range(8):
        sublane = (segment + lead) % 8
        nearer[sublane] = total
        total = total + depth[sublane : sublane + 1]
    through = jnp.exp(-jnp.concatenate([nearer[s] for s in range(8)], axis=0))
    for f in range(3):
        out_ref[f : f + 1, :] = jnp.sum(through * sums[f], axis=0, keepdims=True)
    out_ref[3:4, :] = 1.0 - jnp.exp(-total)


def composite(parts):
    return pl.pallas_call(
        composite_kernel,
        out_shape=jax.ShapeDtypeStruct((4, 128), jnp.float32),
        in_specs=[VMEM],
        out_specs=VMEM,
        compiler_params=pltpu.CompilerParams(vmem_limit_bytes=8 << 20),
        name="composite_chips",
    )(parts)


def solution(mesh):
    devices = mesh.shape["slab"]
    weights = matrices()
    across = [(i, (i + 1) % devices if i % 2 else (i - 1) % devices) for i in range(devices)]
    within = [(i, i ^ 1) for i in range(devices)]
    same_core = [[(2 * (c + TURN) + k) % devices for c in range(devices // 2)] for k in range(2)]

    def edges_of():
        takes, owner = [], {}
        for n, (tiles, image) in enumerate(SEGMENTS):
            owner.update({t % TILES: n for t in tiles})
            need = range(image[0] - 1, image[-1] + 2)
            takes.append(sorted({t % TILES for t in need if owner[t % TILES] != n}))
        hands = [sorted({t for take in takes for t in take if owner[t] == n}) for n in range(len(SEGMENTS))]
        return takes, hands

    takes, hands = edges_of()

    def per_device(velocity):
        x = in_hbm(velocity.reshape(192, NX))
        packed, field_w, line_w = pack([tiles for tiles, _ in SEGMENTS], *map(in_hbm, weights), x)
        from_chip = [lax.ppermute(a, "slab", across) for a, _, _ in packed]
        from_core = [lax.ppermute(b, "slab", within) for _, b, _ in packed]
        edges, swapped = {}, []
        for n, (tiles, image) in enumerate(SEGMENTS):
            keep, send, *handed = slab_image(
                tiles, image, takes[n], hands[n], field_w, line_w, packed[n][2], from_chip[n], from_core[n], *(edges[t] for t in takes[n])
            )
            edges.update(zip(hands[n], handed))
            swapped += [keep, lax.ppermute(send, "slab", within)]
        merged = merge([image for _, image in SEGMENTS], swapped).reshape(128, 4, 128)
        gathered = lax.all_to_all(merged, "slab", 0, 0, axis_index_groups=same_core, tiled=True)
        return composite(gathered.reshape(512, 128))

    return jax.shard_map(per_device, mesh=mesh, in_specs=(P(None, "slab", None, None),), out_specs=P(None, "slab"), check_vma=False)
```

time: 59.8 us -> 47.8 us (0.80)
  Pallas kernels: 10.2 us -> 5.37 us
  blocking collectives: 23.7 us -> 19.8 us
  local copies, waits for them, and re-layouts: 3.3 us -> 0 us
    pallas_call x3, Pallas kernels: 9.43 us -> 4.63 us  [the longest x1 2.32 us: slab_image(): pl.pallas_call(functools.partial(slab_kernel, tiles, image, before, after...]
    all_to_all x1, blocking collectives: 23.7 us -> 19.8 us  [per_device(): lax.all_to_all(merged, 'slab', 0, 0, axis_index_groups=same_core, tiled=T...]
    unnamed x8 -> x0, local copies, waits for them, and re-layouts: 3.3 us -> none
where the time goes in v2:
time: 47.8 us; the launch traced here: 47.7 us
  blocking collectives  19.8 us (41%)
  starting transfers between devices  19.4 us (41%)
  Pallas kernels  5.37 us (11%)
  waiting for transfers between devices  3.07 us (6%)
    all_to_all x1, blocking collectives, per_device(): lax.all_to_all(merged, 'slab', 0, 0, axis_index_groups=same_core, tiled=T...  19.8 us
    ppermute x1, starting transfers between devices, per_device(): from_core = [lax.ppermute(b, 'slab', within) for _, b, _ in packed]  8.76 us
    ppermute x1, starting transfers between devices, per_device(): swapped += [keep, lax.ppermute(send, 'slab', within)]  7.85 us
    ppermute x1, starting transfers between devices, per_device(): from_chip = [lax.ppermute(a, 'slab', across) for a, _, _ in packed]  2.77 us
    pallas_call x1, Pallas kernels, slab_image(): pl.pallas_call(functools.partial(slab_kernel, tiles, image, before, after...  2.32 us
    pallas_call x1, Pallas kernels, pack(): pl.pallas_call(functools.partial(pack_kernel, segments), out_shape=[jax.S...  2.13 us
    ppermute x1, waiting for transfers between devices, per_device(): from_chip = [lax.ppermute(a, 'slab', across) for a, _, _ in packed]  1.21 us
    ppermute x1, waiting for transfers between devices, per_device(): swapped += [keep, lax.ppermute(send, 'slab', within)]  1.16 us
  transfers between devices with their start and end apart: 3, of which 3 were waited for; matrix products, arithmetic and copies ran while one was open for 0% of the time, Pallas kernels for 0%

profile of v2, /device:TPU:1, one launch (start us, length us, event | category | flops | bytes accessed | tf_op | source)
XLA Modules:
  0.0 47.7 jit_solution(4033395431610947965)
XLA Ops:
  0.0 2.1 %pack_halo.1 = (bf16[96,4096]{1,0:T(8,128)(2,1)S(1)}, bf16[96,4096]{1,0:T(8,128)(2,1)S(1)}, bf16[192,4096]{1,0:T(8,128)(2,1)S(1)}, bf16[192,256]{1,0:T(8,128)(2,1)S(1)}, bf16[256,256]{1,0:T(8,128)(2,1)S(1)}) custom-call(bf16[2,192,192]{2,1,0:T(8,128)(2,1)} %constant.6.clone.w_ref, bf16[2,192,256]{2,1,0:T(8,128)(2,1)} %constant.7.clone.f_ref, ...), custom_call_target="tpu_custom_call" | custom-call | tf_op jit(solution)/shard_map/pack_halo/pallas_call | solution.py:179
  2.1 2.8 %collective-permute-start = (bf16[96,4096]{1,0:T(8,128)(2,1)S(1)}, bf16[96,4096]{1,0:T(8,128)(2,1)S(1)}, u32[]{:S(2)}, u32[]{:S(2)}) collective-permute-start(bf16[96,4096]{1,0:T(8,128)(2,1)S(1)} %get-tuple-element.15), channel_id=1, source_target_pairs={{0,255},{1,2},{2,1},{3,4},{4,3},{5,6},{6,5},{7,8},{8,7},{9,10},{10... | collective-permute-start | bytes 2359304 | tf_op jit(solution)/shard_map/ppermute | solution.py:366
  4.9 8.8 %collective-permute-start.1 = (bf16[96,4096]{1,0:T(8,128)(2,1)S(1)}, bf16[96,4096]{1,0:T(8,128)(2,1)S(1)}, u32[]{:S(2)}, u32[]{:S(2)}) collective-permute-start(bf16[96,4096]{1,0:T(8,128)(2,1)S(1)} %get-tuple-element.16), channel_id=1, source_target_pairs={{0,1},{1,0},{2,3},{3,2},{4,5},{5,4},{6,7},{7,6},{8,9},{9,8},{10,11... | collective-permute-start | bytes 2359304 | tf_op jit(solution)/shard_map/ppermute | solution.py:367
  13.7 1.2 %collective-permute-done.refs_3_ = bf16[96,4096]{1,0:T(8,128)(2,1)S(1)} collective-permute-done((bf16[96,4096]{1,0:T(8,128)(2,1)S(1)}, bf16[96,4096]{1,0:T(8,128)(2,1)S(1)}, u32[]{:S(2)}, u32[]{:S(2)}) %collective-permute-start) | collective-permute-done | bytes 786464 | tf_op jit(solution)/shard_map/ppermute | solution.py:366
  14.9 0.7 %collective-permute-done.1.refs_4_ = bf16[96,4096]{1,0:T(8,128)(2,1)S(1)} collective-permute-done((bf16[96,4096]{1,0:T(8,128)(2,1)S(1)}, bf16[96,4096]{1,0:T(8,128)(2,1)S(1)}, u32[]{:S(2)}, u32[]{:S(2)}) %collective-permute-start.1) | collective-permute-done | bytes 786464 | tf_op jit(solution)/shard_map/ppermute | solution.py:367
  15.6 2.3 %slab_image.1 = (f32[512,128]{1,0:T(8,128)S(1)}, f32[512,128]{1,0:T(8,128)S(1)}) custom-call(bf16[192,256]{1,0:T(8,128)(2,1)S(1)} %get-tuple-element.12.refs_0_, bf16[256,256]{1,0:T(8,128)(2,1)S(1)} %get-tuple-element.13.refs_1_, bf16[192,4096]{1,0:T(8,128)(2,1)S(1)} %get-tuple-element.14.refs_2_, bf16[96,4096]{1,0:T(8,128)(2,1)S(1)} %collective-permute-done.refs_3_, ...), custom_call_target="tpu_custom_call" | custom-call | flops 1610612736 | bytes 1048576 | tf_op jit(solution)/shard_map/slab_image/pallas_call | solution.py:269
  17.9 7.9 %collective-permute-start.2 = (f32[512,128]{1,0:T(8,128)S(1)}, f32[512,128]{1,0:T(8,128)S(1)}, u32[]{:S(2)}, u32[]{:S(2)}) collective-permute-start(f32[512,128]{1,0:T(8,128)S(1)} %get-tuple-element.18), channel_id=1, source_target_pairs={{0,1},{1,0},{2,3},{3,2},{4,5},{5,4},{6,7},{7,6},{8,9},{9,8},{10,11... | collective-permute-start | bytes 786440 | tf_op jit(solution)/shard_map/ppermute | solution.py:374
  25.8 1.2 %collective-permute-done.2.refs_1_ = f32[512,128]{1,0:T(8,128)S(1)} collective-permute-done((f32[512,128]{1,0:T(8,128)S(1)}, f32[512,128]{1,0:T(8,128)S(1)}, u32[]{:S(2)}, u32[]{:S(2)}) %collective-permute-start.2) | collective-permute-done | bytes 262176 | tf_op jit(solution)/shard_map/ppermute | solution.py:374
  26.9 0.2 merge_cores.1
  27.1 19.8 %all_to_all.5 = f32[128,4,128]{2,1,0:T(4,128)S(1)} all-to-all(f32[128,4,128]{2,1,0:T(4,128)S(1)} %bitcast.3), channel_id=1, replica_groups={{246,248,250,252,254,0,2,4,6,8,10,12,14,16,18,20,22,24,26,28,30,32,34,3..., dimensions={0} | all-to-all | bytes 524288 | tf_op jit(solution)/shard_map/all_to_all | solution.py:376
  46.9 0.7 %composite_chips.1 = f32[4,128]{1,0:T(4,128)} custom-call(f32[512,128]{1,0:T(8,128)S(1)} %bitcast.4), custom_call_target="tpu_custom_call" | custom-call | tf_op jit(solution)/shard_map/composite_chips/pallas_call | solution.py:335
Async XLA Ops:
  2.1 12.7 %collective-permute-start = (bf16[96,4096]{1,0:T(8,128)(2,1)S(1)}, bf16[96,4096]{1,0:T(8,128)(2,1)S(1)}, u32[]{:S(2)}, u32[]{:S(2)}) collective-permute-start(bf16[96,4096]{1,0:T(8,128)(2,1)S(1)} %get-tuple-element.15), channel_id=1, source_target_pairs={{0,255},{1,2},{2,1},{3,4},{4,3},{5,6},{6,5},{7,8},{8,7},{9,10},{10... | collective-permute-start | bytes 2359304 | tf_op jit(solution)/shard_map/ppermute | solution.py:366
  4.9 10.7 %collective-permute-start.1 = (bf16[96,4096]{1,0:T(8,128)(2,1)S(1)}, bf16[96,4096]{1,0:T(8,128)(2,1)S(1)}, u32[]{:S(2)}, u32[]{:S(2)}) collective-permute-start(bf16[96,4096]{1,0:T(8,128)(2,1)S(1)} %get-tuple-element.16), channel_id=1, source_target_pairs={{0,1},{1,0},{2,3},{3,2},{4,5},{5,4},{6,7},{7,6},{8,9},{9,8},{10,11... | collective-permute-start | bytes 2359304 | tf_op jit(solution)/shard_map/ppermute | solution.py:367
  17.9 9.0 %collective-permute-start.2 = (f32[512,128]{1,0:T(8,128)S(1)}, f32[512,128]{1,0:T(8,128)S(1)}, u32[]{:S(2)}, u32[]{:S(2)}) collective-permute-start(f32[512,128]{1,0:T(8,128)S(1)} %get-tuple-element.18), channel_id=1, source_target_pairs={{0,1},{1,0},{2,3},{3,2},{4,5},{5,4},{6,7},{7,6},{8,9},{9,8},{10,11... | collective-permute-start | bytes 786440 | tf_op jit(solution)/shard_map/ppermute | solution.py:374

commit v3 on v2

v3 whole, which is shorter than its diff:
```python
import numpy as np
import jax
import jax.numpy as jnp
from jax import lax
from jax.experimental import pallas as pl
from jax.experimental.pallas import tpu as pltpu
from jax.sharding import PartitionSpec as P

NX = 4096
TILES = NX // 128
S_INT = {-2: 1, -1: 4, 0: 6, 1: 4, 2: 1}
D_INT = {-2: 1, -1: -8, 1: 8, 2: -1}
DS_INT = {}
for i, a in S_INT.items():
    for j, b in D_INT.items():
        DS_INT[i + j] = DS_INT.get(i + j, 0) + a * b
UX, UY, UZ = 0, 1, 2
OPACITY_GAIN = 5.0


def own_row(c, z, y):
    return (c * 4 + z) * 16 + y


PARTS = ((UX, True, 12), (UX, False, 8), (UY, True, 8), (UY, False, 8), (UZ, True, 12))


def message_rows():
    rows = []
    for c, inner, count in PARTS:
        for k in range(2):
            for i in range(count):
                rows.append((c, inner, k, i + (2 if count == 12 else 4)))
    return rows


def message_plane(inner, k, up):
    return (2 + k if inner else k) if up else (k if inner else 2 + k)


def send_matrix(up):
    w = np.zeros((96, 192), np.float32)
    for n, (c, inner, k, y) in enumerate(message_rows()):
        for dy, t in S_INT.items():
            w[n, own_row(c, message_plane(inner, k, up), y + dy)] += t
    return w


TERMS = (
    (0, UY, "S", "S", 1),
    (1, UZ, "S", "S", 1),
    (2, UZ, "S", "D", 1),
    (2, UY, "D", "S", -1),
    (3, UX, "S", "S", 1),
    (4, UX, "D", "S", 1),
    (5, UX, "S", "D", -1),
)
OWN_YZ, OWN_X, HALO_YZ, HALO_X = slice(64, 192), slice(0, 64), slice(32, 96), slice(0, 48)


def field_matrices():
    own = np.zeros((192, 192), np.float32)
    halo = {False: np.zeros((192, 96), np.float32), True: np.zeros((192, 96), np.float32)}
    place = {up: {} for up in (False, True)}
    for up in (False, True):
        for n, (c, inner, k, y) in enumerate(message_rows()):
            plane = message_plane(inner, k, up) + (-4 if up else 4)
            place[up][c, plane, y] = n
    along = {"S": S_INT, "D": DS_INT}
    for field, c, fz, fy, sign in TERMS:
        for p in range(4):
            for r in range(8):
                m = field * 32 + p * 8 + r
                for dz, a in along[fz].items():
                    q = p + dz
                    if 0 <= q < 4:
                        for dy, b in along[fy].items():
                            own[m, own_row(c, q, r + 4 + dy)] += sign * a * b
                    else:
                        up = q < 0
                        if fy == "S":
                            halo[up][m, place[up][c, q, r + 4]] += sign * a
                        else:
                            for dy, b in D_INT.items():
                                halo[up][m, place[up][c, q, r + 4 + dy]] += sign * a * b
    return own, halo[True], halo[False]


def line_matrix():
    w = np.zeros((256, 256), np.float32)
    for column, taps in ((0, S_INT), (128, DS_INT)):
        for j in range(128):
            for d, t in taps.items():
                row = j + d if 0 <= j + d < 128 else 128 + (j + d) % 128
                w[row, column + j] += t
    return w


def matrices():
    up, down = send_matrix(True), send_matrix(False)
    send = np.stack([np.concatenate([down, up]), np.concatenate([up, down])])
    own, prev, nxt = field_matrices()
    field = np.zeros((2, 192, 256), np.float32)
    for core, halo in enumerate(([prev, nxt], [nxt, prev])):
        field[core, :96] = np.concatenate([own[:96, OWN_YZ], *(h[:96, HALO_YZ] for h in halo)], 1)
        field[core, 96:, :160] = np.concatenate([own[96:, OWN_X], *(h[96:, HALO_X] for h in halo)], 1)
        assert not own[:96, OWN_X].any() and not own[96:, OWN_YZ].any()
        assert not any(h[:96, :32].any() or h[96:, 48:].any() for h in halo)
    return [m.astype(jnp.bfloat16) for m in (send, field, line_matrix())]


PAIRS = TILES // 2
TURN = 123
GROUP = 8
HBM = pl.BlockSpec(memory_space=pltpu.HBM)
VMEM = pl.BlockSpec(memory_space=pltpu.VMEM)


def in_hbm(x):
    return pltpu.with_memory_space_constraint(jnp.asarray(x), pltpu.HBM)


def core_index():
    return lax.rem(lax.axis_index("slab"), 2)


def pack_kernel(w_ref, f_ref, l_ref, x_ref, a_ref, b_ref, xv_ref, fv_ref, lv_ref, wv_ref, sems):
    core = core_index()
    parts = [slice(k * NX // 2, (k + 1) * NX // 2) for k in range(2)]
    sources = [w_ref.at[core]] + [x_ref.at[:, part] for part in parts] + [f_ref.at[core], l_ref]
    targets = [wv_ref] + [xv_ref.at[:, part] for part in parts] + [fv_ref, lv_ref]
    copies = [pltpu.make_async_copy(source, target, sems.at[n]) for n, (source, target) in enumerate(zip(sources, targets))]
    for copy in copies:
        copy.start()
    copies[0].wait()
    for copy, part in zip(copies[1:3], parts):
        copy.wait()
        out = jnp.dot(wv_ref[...], xv_ref[:, part], preferred_element_type=jnp.float32).astype(jnp.bfloat16)
        a_ref[:, part] = out[:96]
        b_ref[:, part] = out[96:]
    for copy in copies[3:]:
        copy.wait()


def pack(*arrays):
    out = [(96, NX), (96, NX), (192, NX), (192, 256), (256, 256)]
    return pl.pallas_call(
        pack_kernel,
        out_shape=[jax.ShapeDtypeStruct(shape, jnp.bfloat16) for shape in out],
        in_specs=[HBM] * 4,
        out_specs=[VMEM] * len(out),
        scratch_shapes=[pltpu.VMEM((192, 192), jnp.bfloat16), pltpu.SemaphoreType.DMA((5,))],
        compiler_params=pltpu.CompilerParams(vmem_limit_bytes=16 << 20),
        name="pack_halo",
    )(*arrays)


def line_image(l_ref, high_ref, low_ref, parity, out_ref):
    half = lax.broadcasted_iota(jnp.int32, (192, 128), 1) < 64

    def line(t):
        previous, here, following = (pl.ds((t + k) % TILES * 128, 128) for k in (-1, 0, 1))
        out = []
        for ref in (high_ref, low_ref):
            out += [ref[:, here], jnp.where(half, ref[:, following], ref[:, previous])]
        return jnp.concatenate(out, axis=1)

    def tile(yz, rest):
        smoothed = [rest[32:64], yz[:32, :128], yz[32:, :128]]
        curl = [rest[:32], rest[64:96] - yz[32:, 128:], rest[96:] + yz[:32, 128:]]
        density = (curl[0] * curl[0] + curl[1] * curl[1] + curl[2] * curl[2]) * (OPACITY_GAIN / 1024.0 / 49152.0**2)
        colours = [0.5 + 0.5 * jnp.tanh(s * (1.0 / 4096.0)) for s in smoothed]
        opacity = 1.0 - jnp.exp(-density)
        depth = density[:8]
        weight = opacity[:8]
        sums = [weight * c[:8] for c in colours]
        for p in range(1, 4):
            part = slice(8 * p, 8 * p + 8)
            weight = jnp.exp(-depth) * opacity[part]
            sums = [s + weight * c[part] for s, c in zip(sums, colours)]
            depth = depth + density[part]
        return sums + [depth]

    both = jnp.concatenate([l_ref[...]] * 2, axis=0)
    for first in range(0, PAIRS, GROUP):
        lines = [line(2 * (first + n) + parity) for n in range(GROUP)]
        yz = jnp.dot(jnp.concatenate([v[:64] for v in lines], axis=0), both, preferred_element_type=jnp.float32)
        rest = jnp.dot(jnp.concatenate([v[64:] for v in lines], axis=0), both[:, :128], preferred_element_type=jnp.float32)
        for n in range(GROUP):
            for f, value in enumerate(tile(yz[n * 64 : n * 64 + 64], rest[n * 128 : n * 128 + 128])):
                row = (f * PAIRS + first + n) * 8
                out_ref[row : row + 8, :] = value


def first_image_kernel(w_ref, l_ref, x_ref, a_ref, b_ref, send_ref, high_ref, low_ref):
    for n in range(0, NX, 256):
        cols = slice(n, n + 256)
        yz = jnp.concatenate([x_ref[OWN_YZ, cols], a_ref[HALO_YZ, cols], b_ref[HALO_YZ, cols]], axis=0)
        x = jnp.concatenate([x_ref[OWN_X, cols], a_ref[HALO_X, cols], b_ref[HALO_X, cols]], axis=0)
        out = jnp.concatenate(
            [
                jnp.dot(w_ref[:96, :], yz, preferred_element_type=jnp.float32),
                jnp.dot(w_ref[96:, :160], x, preferred_element_type=jnp.float32),
            ],
            axis=0,
        )
        high = out.astype(jnp.bfloat16)
        high_ref[:, cols] = high
        low_ref[:, cols] = (out - high.astype(jnp.float32)).astype(jnp.bfloat16)
    core = core_index()
    for parity in range(2):

        @pl.when(core == 1 - parity)
        def _(parity=parity):
            line_image(l_ref, high_ref, low_ref, parity, send_ref)


def second_image_kernel(l_ref, high_ref, low_ref, keep_ref):
    core = core_index()
    for parity in range(2):

        @pl.when(core == parity)
        def _(parity=parity):
            line_image(l_ref, high_ref, low_ref, parity, keep_ref)


def image_call(kernel, name, outs, *arrays):
    return pl.pallas_call(
        kernel,
        out_shape=outs,
        in_specs=[VMEM] * len(arrays),
        out_specs=[VMEM] * len(outs),
        compiler_params=pltpu.CompilerParams(vmem_limit_bytes=16 << 20),
        cost_estimate=pl.CostEstimate(flops=2 * 192 * 1024 * NX, bytes_accessed=1 << 20, transcendentals=0),
        name=name,
    )(*arrays)


def first_image(*arrays):
    image, field = jax.ShapeDtypeStruct((PAIRS * 32, 128), jnp.float32), jax.ShapeDtypeStruct((192, NX), jnp.bfloat16)
    return image_call(first_image_kernel, "send_image", [image, field, field], *arrays)


def second_image(*arrays):
    image = jax.ShapeDtypeStruct((PAIRS * 32, 128), jnp.float32)
    return image_call(second_image_kernel, "keep_image", [image], *arrays)[0]


def merge_kernel(own_ref, other_ref, out_ref):
    first = core_index() == 0
    own, other = ([ref[f * PAIRS * 8 : (f + 1) * PAIRS * 8, :] for f in range(4)] for ref in (own_ref, other_ref))
    zero = jnp.zeros_like(own[3])
    own_scale = jnp.exp(-jnp.where(first, zero, other[3]))
    other_scale = jnp.exp(-jnp.where(first, own[3], zero))
    merged = [own_scale * a + other_scale * b for a, b in zip(own[:3], other[:3])] + [own[3] + other[3]]
    for f in range(4):
        for pair in range(PAIRS):
            rank = (pair - TURN) % 128
            value, turn = merged[f][pair * 8 : pair * 8 + 8], rank // 16
            out_ref[pl.ds(rank % 16 * 4 + f, 8, stride=64), :] = pltpu.roll(value, turn, 0) if turn else value


def merge(own, other):
    return pl.pallas_call(
        merge_kernel,
        out_shape=jax.ShapeDtypeStruct((512, 128), jnp.float32),
        in_specs=[VMEM] * 2,
        out_specs=VMEM,
        compiler_params=pltpu.CompilerParams(vmem_limit_bytes=8 << 20),
        name="merge_cores",
    )(own, other)


def composite_kernel(in_ref, out_ref):
    lead = (-TURN) % 128 // 16

    def part(v, f):
        rank = (v - TURN) % 128
        value = in_ref[pl.ds(rank % 16 * 4 + f, 8, stride=64), :]
        turn = (lead - rank // 16) % 8
        return pltpu.roll(value, turn, 0) if turn else value

    depth = part(0, 3)
    sums = [part(0, f) for f in range(3)]
    for v in range(1, 16):
        through = jnp.exp(-depth)
        sums = [s + through * part(v, f) for f, s in enumerate(sums)]
        depth = depth + part(v, 3)
    nearer, total = {}, jnp.zeros((1, 128), jnp.float32)
    for segment in range(8):
        sublane = (segment + lead) % 8
        nearer[sublane] = total
        total = total + depth[sublane : sublane + 1]
    through = jnp.exp(-jnp.concatenate([nearer[s] for s in range(8)], axis=0))
    for f in range(3):
        out_ref[f : f + 1, :] = jnp.sum(through * sums[f], axis=0, keepdims=True)
    out_ref[3:4, :] = 1.0 - jnp.exp(-total)


def composite(parts):
    return pl.pallas_call(
        composite_kernel,
        out_shape=jax.ShapeDtypeStruct((4, 128), jnp.float32),
        in_specs=[VMEM],
        out_specs=VMEM,
        compiler_params=pltpu.CompilerParams(vmem_limit_bytes=8 << 20),
        name="composite_chips",
    )(parts)


def solution(mesh):
    devices = mesh.shape["slab"]
    weights = matrices()
    across = [(i, (i + 1) % devices if i % 2 else (i - 1) % devices) for i in range(devices)]
    within = [(i, i ^ 1) for i in range(devices)]
    same_core = [[(2 * (c + TURN) + k) % devices for c in range(devices // 2)] for k in range(2)]

    def per_device(velocity):
        x = in_hbm(velocity.reshape(192, NX))
        to_chip, to_core, x, field_w, line_w = pack(*map(in_hbm, weights), x)
        from_chip = lax.ppermute(to_chip, "slab", across)
        from_core = lax.ppermute(to_core, "slab", within)
        send, high, low = first_image(field_w, line_w, x, from_chip, from_core)
        other = lax.ppermute(send, "slab", within)
        keep = second_image(line_w, high, low)
        merged = merge(keep, other).reshape(128, 4, 128)
        gathered = lax.all_to_all(merged, "slab", 0, 0, axis_index_groups=same_core, tiled=True)
        return composite(gathered.reshape(512, 128))

    return jax.shard_map(per_device, mesh=mesh, in_specs=(P(None, "slab", None, None),), out_specs=P(None, "slab"), check_vma=False)
```

time: 47.8 us -> 47.1 us (0.985)
  waiting for transfers between devices: 3.07 us -> 2.06 us
    ppermute x3, waiting for transfers between devices: 3.07 us -> 2.06 us  [the longest x1 1.21 us: per_device(): from_chip = lax.ppermute(to_chip, 'slab', across)]
    pallas_call x3 -> x4, Pallas kernels: 4.63 us -> 4.92 us  [the longest x2 2.77 us: image_call(): pl.pallas_call(kernel, out_shape=outs, in_specs=[VMEM] * len(arrays), out...]
  transfers between devices with their start and end apart: 3 -> 3, of which waited for: 3 -> 3; matrix products, arithmetic and copies ran while one was open for 0% -> 0% of each run, Pallas kernels for 0% -> 2%
where the time goes in v3:
time: 47.1 us; the launch traced here: 47 us
  blocking collectives  19.8 us (42%)
  starting transfers between devices  19.4 us (41%)
  Pallas kernels  5.66 us (12%)
  waiting for transfers between devices  2.06 us (4%)
    all_to_all x1, blocking collectives, per_device(): lax.all_to_all(merged, 'slab', 0, 0, axis_index_groups=same_core, tiled=T...  19.8 us
    ppermute x1, starting transfers between devices, per_device(): from_core = lax.ppermute(to_core, 'slab', within)  8.76 us
    ppermute x1, starting transfers between devices, per_device(): other = lax.ppermute(send, 'slab', within)  7.85 us
    pallas_call x2, Pallas kernels, image_call(): pl.pallas_call(kernel, out_shape=outs, in_specs=[VMEM] * len(arrays), out...  2.77 us
    ppermute x1, starting transfers between devices, per_device(): from_chip = lax.ppermute(to_chip, 'slab', across)  2.77 us
    pallas_call x1, Pallas kernels, pack(): pl.pallas_call(pack_kernel, out_shape=[jax.ShapeDtypeStruct(shape, jnp.bf...  1.96 us
    ppermute x1, waiting for transfers between devices, per_device(): from_chip = lax.ppermute(to_chip, 'slab', across)  1.21 us
  transfers between devices with their start and end apart: 3, of which 3 were waited for; matrix products, arithmetic and copies ran while one was open for 0% of the time, Pallas kernels for 2%

profile of v3, /device:TPU:1, one launch (start us, length us, event | category | flops | bytes accessed | tf_op | source)
XLA Modules:
  0.0 47.0 jit_solution(9523948005225573441)
XLA Ops:
  0.0 2.0 %pack_halo.1 = (bf16[96,4096]{1,0:T(8,128)(2,1)S(1)}, bf16[96,4096]{1,0:T(8,128)(2,1)S(1)}, bf16[192,4096]{1,0:T(8,128)(2,1)S(1)}, bf16[192,256]{1,0:T(8,128)(2,1)S(1)}, bf16[256,256]{1,0:T(8,128)(2,1)S(1)}) custom-call(bf16[2,192,192]{2,1,0:T(8,128)(2,1)} %constant.6.clone.w_ref, bf16[2,192,256]{2,1,0:T(8,128)(2,1)} %constant.7.clone.f_ref, ...), custom_call_target="tpu_custom_call" | custom-call | tf_op jit(solution)/shard_map/pack_halo/pallas_call | solution.py:147
  2.0 2.8 %collective-permute-start = (bf16[96,4096]{1,0:T(8,128)(2,1)S(1)}, bf16[96,4096]{1,0:T(8,128)(2,1)S(1)}, u32[]{:S(2)}, u32[]{:S(2)}) collective-permute-start(bf16[96,4096]{1,0:T(8,128)(2,1)S(1)} %get-tuple-element.16), channel_id=1, source_target_pairs={{0,255},{1,2},{2,1},{3,4},{4,3},{5,6},{6,5},{7,8},{8,7},{9,10},{10... | collective-permute-start | bytes 2359304 | tf_op jit(solution)/shard_map/ppermute | solution.py:321
  4.7 8.8 %collective-permute-start.1 = (bf16[96,4096]{1,0:T(8,128)(2,1)S(1)}, bf16[96,4096]{1,0:T(8,128)(2,1)S(1)}, u32[]{:S(2)}, u32[]{:S(2)}) collective-permute-start(bf16[96,4096]{1,0:T(8,128)(2,1)S(1)} %get-tuple-element.17), channel_id=1, source_target_pairs={{0,1},{1,0},{2,3},{3,2},{4,5},{5,4},{6,7},{7,6},{8,9},{9,8},{10,11... | collective-permute-start | bytes 2359304 | tf_op jit(solution)/shard_map/ppermute | solution.py:322
  13.5 1.2 %collective-permute-done.a_ref = bf16[96,4096]{1,0:T(8,128)(2,1)S(1)} collective-permute-done((bf16[96,4096]{1,0:T(8,128)(2,1)S(1)}, bf16[96,4096]{1,0:T(8,128)(2,1)S(1)}, u32[]{:S(2)}, u32[]{:S(2)}) %collective-permute-start) | collective-permute-done | bytes 786464 | tf_op jit(solution)/shard_map/ppermute | solution.py:321
  14.7 0.7 %collective-permute-done.1.b_ref = bf16[96,4096]{1,0:T(8,128)(2,1)S(1)} collective-permute-done((bf16[96,4096]{1,0:T(8,128)(2,1)S(1)}, bf16[96,4096]{1,0:T(8,128)(2,1)S(1)}, u32[]{:S(2)}, u32[]{:S(2)}) %collective-permute-start.1) | collective-permute-done | bytes 786464 | tf_op jit(solution)/shard_map/ppermute | solution.py:322
  15.4 1.8 %send_image.1 = (f32[512,128]{1,0:T(8,128)S(1)}, bf16[192,4096]{1,0:T(8,128)(2,1)S(1)}, bf16[192,4096]{1,0:T(8,128)(2,1)S(1)}) custom-call(bf16[192,256]{1,0:T(8,128)(2,1)S(1)} %get-tuple-element.14.w_ref, bf16[256,256]{1,0:T(8,128)(2,1)S(1)} %get-tuple-element.13.l_ref, bf16[192,4096]{1,0:T(8,128)(2,1)S(1)} %get-tuple-element.15.x_ref, ...), custom_call_target="tpu_custom_call" | custom-call | flops 1610612736 | bytes 1048576 | tf_op jit(solution)/shard_map/send_image/pallas_call | solution.py:228
  17.2 7.8 %collective-permute-start.2 = (f32[512,128]{1,0:T(8,128)S(1)}, f32[512,128]{1,0:T(8,128)S(1)}, u32[]{:S(2)}, u32[]{:S(2)}) collective-permute-start(f32[512,128]{1,0:T(8,128)S(1)} %get-tuple-element.20), channel_id=1, source_target_pairs={{0,1},{1,0},{2,3},{3,2},{4,5},{5,4},{6,7},{7,6},{8,9},{9,8},{10,11... | collective-permute-start | bytes 786440 | tf_op jit(solution)/shard_map/ppermute | solution.py:324
  25.0 1.0 %keep_image.1.own_ref = f32[512,128]{1,0:T(8,128)S(1)} custom-call(bf16[256,256]{1,0:T(8,128)(2,1)S(1)} %get-tuple-element.13.l_ref, bf16[192,4096]{1,0:T(8,128)(2,1)S(1)} %get-tuple-element.18.high_ref, bf16[192,4096]{1,0:T(8,128)(2,1)S(1)} %get-tuple-element.19.low_ref), custom_call_target="tpu_custom_call" | custom-call | flops 1610612736 | bytes 1048576 | tf_op jit(solution)/shard_map/keep_image/pallas_call | solution.py:228
  26.1 0.1 collective-permute-done.2.other_ref
  26.2 0.2 merge_cores.1
  26.4 19.8 %all_to_all.5 = f32[128,4,128]{2,1,0:T(4,128)S(1)} all-to-all(f32[128,4,128]{2,1,0:T(4,128)S(1)} %bitcast.3), channel_id=1, replica_groups={{246,248,250,252,254,0,2,4,6,8,10,12,14,16,18,20,22,24,26,28,30,32,34,3..., dimensions={0} | all-to-all | bytes 524288 | tf_op jit(solution)/shard_map/all_to_all | solution.py:327
  46.2 0.7 %composite_chips.1 = f32[4,128]{1,0:T(4,128)} custom-call(f32[512,128]{1,0:T(8,128)S(1)} %bitcast.4), custom_call_target="tpu_custom_call" | custom-call | tf_op jit(solution)/shard_map/composite_chips/pallas_call | solution.py:301
Async XLA Ops:
  2.0 12.7 %collective-permute-start = (bf16[96,4096]{1,0:T(8,128)(2,1)S(1)}, bf16[96,4096]{1,0:T(8,128)(2,1)S(1)}, u32[]{:S(2)}, u32[]{:S(2)}) collective-permute-start(bf16[96,4096]{1,0:T(8,128)(2,1)S(1)} %get-tuple-element.16), channel_id=1, source_target_pairs={{0,255},{1,2},{2,1},{3,4},{4,3},{5,6},{6,5},{7,8},{8,7},{9,10},{10... | collective-permute-start | bytes 2359304 | tf_op jit(solution)/shard_map/ppermute | solution.py:321
  4.7 10.7 %collective-permute-start.1 = (bf16[96,4096]{1,0:T(8,128)(2,1)S(1)}, bf16[96,4096]{1,0:T(8,128)(2,1)S(1)}, u32[]{:S(2)}, u32[]{:S(2)}) collective-permute-start(bf16[96,4096]{1,0:T(8,128)(2,1)S(1)} %get-tuple-element.17), channel_id=1, source_target_pairs={{0,1},{1,0},{2,3},{3,2},{4,5},{5,4},{6,7},{7,6},{8,9},{9,8},{10,11... | collective-permute-start | bytes 2359304 | tf_op jit(solution)/shard_map/ppermute | solution.py:322
  17.2 9.0 %collective-permute-start.2 = (f32[512,128]{1,0:T(8,128)S(1)}, f32[512,128]{1,0:T(8,128)S(1)}, u32[]{:S(2)}, u32[]{:S(2)}) collective-permute-start(f32[512,128]{1,0:T(8,128)S(1)} %get-tuple-element.20), channel_id=1, source_target_pairs={{0,1},{1,0},{2,3},{3,2},{4,5},{5,4},{6,7},{7,6},{8,9},{9,8},{10,11... | collective-permute-start | bytes 786440 | tf_op jit(solution)/shard_map/ppermute | solution.py:324

commit v4 on v3

--- a/solution.py
+++ b/solution.py
@@ -110,7 +110,7 @@
 
 
 PAIRS = TILES // 2
-TURN = 123
+TURN = 122
 GROUP = 8
 HBM = pl.BlockSpec(memory_space=pltpu.HBM)
 VMEM = pl.BlockSpec(memory_space=pltpu.VMEM)
@@ -124,7 +124,7 @@
     return lax.rem(lax.axis_index("slab"), 2)
 
 
-def pack_kernel(w_ref, f_ref, l_ref, x_ref, a_ref, b_ref, xv_ref, fv_ref, lv_ref, wv_ref, sems):
+def pack_kernel(w_ref, f_ref, l_ref, x_ref, a_ref, xv_ref, wv_ref, fv_ref, lv_ref, sems):
     core = core_index()
     parts = [slice(k * NX // 2, (k + 1) * NX // 2) for k in range(2)]
     sources = [w_ref.at[core]] + [x_ref.at[:, part] for part in parts] + [f_ref.at[core], l_ref]
@@ -135,24 +135,31 @@
     copies[0].wait()
     for copy, part in zip(copies[1:3], parts):
         copy.wait()
-        out = jnp.dot(wv_ref[...], xv_ref[:, part], preferred_element_type=jnp.float32).astype(jnp.bfloat16)
-        a_ref[:, part] = out[:96]
-        b_ref[:, part] = out[96:]
+        a_ref[:, part] = jnp.dot(wv_ref[:96, :], xv_ref[:, part], preferred_element_type=jnp.float32).astype(jnp.bfloat16)
     for copy in copies[3:]:
         copy.wait()
 
 
 def pack(*arrays):
-    out = [(96, NX), (96, NX), (192, NX), (192, 256), (256, 256)]
+    out = [(96, NX), (192, NX), (192, 192), (192, 256), (256, 256)]
     return pl.pallas_call(
         pack_kernel,
         out_shape=[jax.ShapeDtypeStruct(shape, jnp.bfloat16) for shape in out],
         in_specs=[HBM] * 4,
         out_specs=[VMEM] * len(out),
-        scratch_shapes=[pltpu.VMEM((192, 192), jnp.bfloat16), pltpu.SemaphoreType.DMA((5,))],
+        scratch_shapes=[pltpu.SemaphoreType.DMA((5,))],
         compiler_params=pltpu.CompilerParams(vmem_limit_bytes=16 << 20),
         name="pack_halo",
     )(*arrays)
+
+
+def pack_core_kernel(w_ref, x_ref, *b_refs):
+    for part, b_ref in zip((slice(0, NX // 2), slice(NX // 2, NX)), b_refs):
+        b_ref[...] = jnp.dot(w_ref[96:, :], x_ref[:, part], preferred_element_type=jnp.float32).astype(jnp.bfloat16)
+
+
+def pack_core(*arrays):
+    return image_call(pack_core_kernel, "pack_core", [jax.ShapeDtypeStruct((96, NX // 2), jnp.bfloat16)] * 2, *arrays)
 
 
 def line_image(l_ref, high_ref, low_ref, parity, out_ref):
@@ -192,26 +199,30 @@
                 out_ref[row : row + 8, :] = value
 
 
-def first_image_kernel(w_ref, l_ref, x_ref, a_ref, b_ref, send_ref, high_ref, low_ref):
-    for n in range(0, NX, 256):
-        cols = slice(n, n + 256)
-        yz = jnp.concatenate([x_ref[OWN_YZ, cols], a_ref[HALO_YZ, cols], b_ref[HALO_YZ, cols]], axis=0)
-        x = jnp.concatenate([x_ref[OWN_X, cols], a_ref[HALO_X, cols], b_ref[HALO_X, cols]], axis=0)
-        out = jnp.concatenate(
-            [
-                jnp.dot(w_ref[:96, :], yz, preferred_element_type=jnp.float32),
-                jnp.dot(w_ref[96:, :160], x, preferred_element_type=jnp.float32),
-            ],
-            axis=0,
-        )
-        high = out.astype(jnp.bfloat16)
-        high_ref[:, cols] = high
-        low_ref[:, cols] = (out - high.astype(jnp.float32)).astype(jnp.bfloat16)
+def zy_fields(w_ref, x_ref, a_ref, b_ref, high_ref, low_ref, cols):
+    half = slice(cols.start % (NX // 2), cols.start % (NX // 2) + cols.stop - cols.start)
+    yz = jnp.concatenate([x_ref[OWN_YZ, cols], a_ref[HALO_YZ, cols], b_ref[HALO_YZ, half]], axis=0)
+    x = jnp.concatenate([x_ref[OWN_X, cols], a_ref[HALO_X, cols], b_ref[HALO_X, half]], axis=0)
+    out = jnp.concatenate(
+        [
+            jnp.dot(w_ref[:96, :], yz, preferred_element_type=jnp.float32),
+            jnp.dot(w_ref[96:, :160], x, preferred_element_type=jnp.float32),
+        ],
+        axis=0,
+    )
+    high = out.astype(jnp.bfloat16)
+    high_ref[:, cols] = high
+    low_ref[:, cols] = (out - high.astype(jnp.float32)).astype(jnp.bfloat16)
+
+
+def first_image_kernel(w_ref, l_ref, x_ref, a_ref, b0_ref, b1_ref, send_ref, high_ref, low_ref):
     core = core_index()
     for parity in range(2):
 
         @pl.when(core == 1 - parity)
         def _(parity=parity):
+            for n in range(0, NX, 512):
+                zy_fields(w_ref, x_ref, a_ref, (b0_ref, b1_ref)[n // (NX // 2)], high_ref, low_ref, slice(n, n + 512))
             line_image(l_ref, high_ref, low_ref, parity, send_ref)
 
 
@@ -317,10 +328,10 @@
 
     def per_device(velocity):
         x = in_hbm(velocity.reshape(192, NX))
-        to_chip, to_core, x, field_w, line_w = pack(*map(in_hbm, weights), x)
+        to_chip, x, send_w, field_w, line_w = pack(*map(in_hbm, weights), x)
         from_chip = lax.ppermute(to_chip, "slab", across)
-        from_core = lax.ppermute(to_core, "slab", within)
-        send, high, low = first_image(field_w, line_w, x, from_chip, from_core)
+        from_core = [lax.ppermute(part, "slab", within) for part in pack_core(send_w, x)]
+        send, high, low = first_image(field_w, line_w, x, from_chip, *from_core)
         other = lax.ppermute(send, "slab", within)
         keep = second_image(line_w, high, low)
         merged = merge(keep, other).reshape(128, 4, 128)

time: 47.1 us -> 46.8 us (level)
    ppermute x1, waiting for transfers between devices: 1.21 us -> 0.01 us  [per_device(): from_chip = lax.ppermute(to_chip, 'slab', across)]
    ppermute x1 -> x2, waiting for transfers between devices: 0.7 us -> 1.81 us  [per_device(): lax.ppermute(part, 'slab', within)]
    ppermute x1, starting transfers between devices: 7.85 us -> 7.35 us  [per_device(): other = lax.ppermute(send, 'slab', within)]
    pallas_call x2 -> x3, Pallas kernels: 2.77 us -> 3.06 us  [image_call(): pl.pallas_call(kernel, out_shape=outs, in_specs=[VMEM] * len(arrays), out...]
    ppermute x1 -> x2, starting transfers between devices: 8.76 us -> 8.94 us  [per_device(): lax.ppermute(part, 'slab', within)]
  transfers between devices with their start and end apart: 3 -> 4, of which waited for: 3 -> 3; matrix products, arithmetic and copies ran while one was open for 0% -> 0% of each run, Pallas kernels for 2% -> 3%
where the time goes in v4:
time: 46.8 us; the launch traced here: 46.7 us
  blocking collectives  19.9 us (43%)
  starting transfers between devices  19.1 us (41%)
  Pallas kernels  5.75 us (12%)
  waiting for transfers between devices  1.96 us (4%)
    all_to_all x1, blocking collectives, per_device(): lax.all_to_all(merged, 'slab', 0, 0, axis_index_groups=same_core, tiled=T...  19.9 us
    ppermute x2, starting transfers between devices, per_device(): lax.ppermute(part, 'slab', within)  8.94 us
    ppermute x1, starting transfers between devices, per_device(): other = lax.ppermute(send, 'slab', within)  7.35 us
    pallas_call x3, Pallas kernels, image_call(): pl.pallas_call(kernel, out_shape=outs, in_specs=[VMEM] * len(arrays), out...  3.06 us
    ppermute x1, starting transfers between devices, per_device(): from_chip = lax.ppermute(to_chip, 'slab', across)  2.77 us
    ppermute x2, waiting for transfers between devices, per_device(): lax.ppermute(part, 'slab', within)  1.81 us
    pallas_call x1, Pallas kernels, pack(): pl.pallas_call(pack_kernel, out_shape=[jax.ShapeDtypeStruct(shape, jnp.bf...  1.78 us
  transfers between devices with their start and end apart: 4, of which 3 were waited for; matrix products, arithmetic and copies ran while one was open for 0% of the time, Pallas kernels for 3%

profile of v4, /device:TPU:1, one launch (start us, length us, event | category | flops | bytes accessed | tf_op | source)
XLA Modules:
  0.0 46.7 jit_solution(18287161852889934333)
XLA Ops:
  0.0 1.8 %pack_halo.1 = (bf16[96,4096]{1,0:T(8,128)(2,1)S(1)}, bf16[192,4096]{1,0:T(8,128)(2,1)S(1)}, bf16[192,192]{1,0:T(8,128)(2,1)S(1)}, bf16[192,256]{1,0:T(8,128)(2,1)S(1)}, bf16[256,256]{1,0:T(8,128)(2,1)S(1)}) custom-call(bf16[2,192,192]{2,1,0:T(8,128)(2,1)} %constant.6.clone.w_ref, bf16[2,192,256]{2,1,0:T(8,128)(2,1)} %constant.7.clone.f_ref, ...), custom_call_target="tpu_custom_call" | custom-call | tf_op jit(solution)/shard_map/pack_halo/pallas_call | solution.py:145
  1.8 2.8 %collective-permute-start = (bf16[96,4096]{1,0:T(8,128)(2,1)S(1)}, bf16[96,4096]{1,0:T(8,128)(2,1)S(1)}, u32[]{:S(2)}, u32[]{:S(2)}) collective-permute-start(bf16[96,4096]{1,0:T(8,128)(2,1)S(1)} %get-tuple-element.18), channel_id=1, source_target_pairs={{0,255},{1,2},{2,1},{3,4},{4,3},{5,6},{6,5},{7,8},{8,7},{9,10},{10... | collective-permute-start | bytes 2359304 | tf_op jit(solution)/shard_map/ppermute | solution.py:332
  4.6 0.4 pack_core.1
  4.9 8.8 %collective-permute-start.1 = (bf16[96,2048]{1,0:T(8,128)(2,1)S(1)}, bf16[96,2048]{1,0:T(8,128)(2,1)S(1)}, u32[]{:S(2)}, u32[]{:S(2)}) collective-permute-start(bf16[96,2048]{1,0:T(8,128)(2,1)S(1)} %get-tuple-element.20), channel_id=1, source_target_pairs={{0,1},{1,0},{2,3},{3,2},{4,5},{5,4},{6,7},{7,6},{8,9},{9,8},{10,11... | collective-permute-start | bytes 1179656 | tf_op jit(solution)/shard_map/ppermute | solution.py:333
  13.8 0.1 collective-permute-start.2
  13.9 1.2 %collective-permute-done.1.b0_ref = bf16[96,2048]{1,0:T(8,128)(2,1)S(1)} collective-permute-done((bf16[96,2048]{1,0:T(8,128)(2,1)S(1)}, bf16[96,2048]{1,0:T(8,128)(2,1)S(1)}, u32[]{:S(2)}, u32[]{:S(2)}) %collective-permute-start.1) | collective-permute-done | bytes 393248 | tf_op jit(solution)/shard_map/ppermute | solution.py:333
  15.1 0.6 %collective-permute-done.2.b1_ref = bf16[96,2048]{1,0:T(8,128)(2,1)S(1)} collective-permute-done((bf16[96,2048]{1,0:T(8,128)(2,1)S(1)}, bf16[96,2048]{1,0:T(8,128)(2,1)S(1)}, u32[]{:S(2)}, u32[]{:S(2)}) %collective-permute-start.2) | collective-permute-done | bytes 393248 | tf_op jit(solution)/shard_map/ppermute | solution.py:333
  15.7 0.0 collective-permute-done.a_ref
  15.7 1.7 %send_image.1 = (f32[512,128]{1,0:T(8,128)S(1)}, bf16[192,4096]{1,0:T(8,128)(2,1)S(1)}, bf16[192,4096]{1,0:T(8,128)(2,1)S(1)}) custom-call(bf16[192,256]{1,0:T(8,128)(2,1)S(1)} %get-tuple-element.16.w_ref, bf16[256,256]{1,0:T(8,128)(2,1)S(1)} %get-tuple-element.15.l_ref, bf16[192,4096]{1,0:T(8,128)(2,1)S(1)} %get-tuple-element.17.x_ref, ...), custom_call_target="tpu_custom_call" | custom-call | flops 1610612736 | bytes 1048576 | tf_op jit(solution)/shard_map/send_image/pallas_call | solution.py:239
  17.4 7.4 %collective-permute-start.3 = (f32[512,128]{1,0:T(8,128)S(1)}, f32[512,128]{1,0:T(8,128)S(1)}, u32[]{:S(2)}, u32[]{:S(2)}) collective-permute-start(f32[512,128]{1,0:T(8,128)S(1)} %get-tuple-element.24), channel_id=1, source_target_pairs={{0,1},{1,0},{2,3},{3,2},{4,5},{5,4},{6,7},{7,6},{8,9},{9,8},{10,11... | collective-permute-start | bytes 786440 | tf_op jit(solution)/shard_map/ppermute | solution.py:335
  24.7 1.0 %keep_image.1.own_ref = f32[512,128]{1,0:T(8,128)S(1)} custom-call(bf16[256,256]{1,0:T(8,128)(2,1)S(1)} %get-tuple-element.15.l_ref, bf16[192,4096]{1,0:T(8,128)(2,1)S(1)} %get-tuple-element.22.high_ref, bf16[192,4096]{1,0:T(8,128)(2,1)S(1)} %get-tuple-element.23.low_ref), custom_call_target="tpu_custom_call" | custom-call | flops 1610612736 | bytes 1048576 | tf_op jit(solution)/shard_map/keep_image/pallas_call | solution.py:239
  25.8 0.1 collective-permute-done.3.other_ref
  25.9 0.2 merge_cores.1
  26.1 19.9 %all_to_all.5 = f32[128,4,128]{2,1,0:T(4,128)S(1)} all-to-all(f32[128,4,128]{2,1,0:T(4,128)S(1)} %bitcast.3), channel_id=1, replica_groups={{244,246,248,250,252,254,0,2,4,6,8,10,12,14,16,18,20,22,24,26,28,30,32,..., dimensions={0} | all-to-all | bytes 524288 | tf_op jit(solution)/shard_map/all_to_all | solution.py:338
  45.9 0.7 %composite_chips.1 = f32[4,128]{1,0:T(4,128)} custom-call(f32[512,128]{1,0:T(8,128)S(1)} %bitcast.4), custom_call_target="tpu_custom_call" | custom-call | tf_op jit(solution)/shard_map/composite_chips/pallas_call | solution.py:312
Async XLA Ops:
  1.8 13.9 %collective-permute-start = (bf16[96,4096]{1,0:T(8,128)(2,1)S(1)}, bf16[96,4096]{1,0:T(8,128)(2,1)S(1)}, u32[]{:S(2)}, u32[]{:S(2)}) collective-permute-start(bf16[96,4096]{1,0:T(8,128)(2,1)S(1)} %get-tuple-element.18), channel_id=1, source_target_pairs={{0,255},{1,2},{2,1},{3,4},{4,3},{5,6},{6,5},{7,8},{8,7},{9,10},{10... | collective-permute-start | bytes 2359304 | tf_op jit(solution)/shard_map/ppermute | solution.py:332
  4.9 10.2 %collective-permute-start.1 = (bf16[96,2048]{1,0:T(8,128)(2,1)S(1)}, bf16[96,2048]{1,0:T(8,128)(2,1)S(1)}, u32[]{:S(2)}, u32[]{:S(2)}) collective-permute-start(bf16[96,2048]{1,0:T(8,128)(2,1)S(1)} %get-tuple-element.20), channel_id=1, source_target_pairs={{0,1},{1,0},{2,3},{3,2},{4,5},{5,4},{6,7},{7,6},{8,9},{9,8},{10,11... | collective-permute-start | bytes 1179656 | tf_op jit(solution)/shard_map/ppermute | solution.py:333
  13.8 1.9 %collective-permute-start.2 = (bf16[96,2048]{1,0:T(8,128)(2,1)S(1)}, bf16[96,2048]{1,0:T(8,128)(2,1)S(1)}, u32[]{:S(2)}, u32[]{:S(2)}) collective-permute-start(bf16[96,2048]{1,0:T(8,128)(2,1)S(1)} %get-tuple-element.21), channel_id=1, source_target_pairs={{0,1},{1,0},{2,3},{3,2},{4,5},{5,4},{6,7},{7,6},{8,9},{9,8},{10,11... | collective-permute-start | bytes 1179656 | tf_op jit(solution)/shard_map/ppermute | solution.py:333
  17.4 8.5 %collective-permute-start.3 = (f32[512,128]{1,0:T(8,128)S(1)}, f32[512,128]{1,0:T(8,128)S(1)}, u32[]{:S(2)}, u32[]{:S(2)}) collective-permute-start(f32[512,128]{1,0:T(8,128)S(1)} %get-tuple-element.24), channel_id=1, source_target_pairs={{0,1},{1,0},{2,3},{3,2},{4,5},{5,4},{6,7},{7,6},{8,9},{9,8},{10,11... | collective-permute-start | bytes 786440 | tf_op jit(solution)/shard_map/ppermute | solution.py:335

commit v5 on v4

--- a/solution.py
+++ b/solution.py
@@ -100,17 +100,18 @@
     up, down = send_matrix(True), send_matrix(False)
     send = np.stack([np.concatenate([down, up]), np.concatenate([up, down])])
     own, prev, nxt = field_matrices()
-    field = np.zeros((2, 192, 256), np.float32)
-    for core, halo in enumerate(([prev, nxt], [nxt, prev])):
-        field[core, :96] = np.concatenate([own[:96, OWN_YZ], *(h[:96, HALO_YZ] for h in halo)], 1)
-        field[core, 96:, :160] = np.concatenate([own[96:, OWN_X], *(h[96:, HALO_X] for h in halo)], 1)
+    field = np.zeros((2, 192, 384), np.float32)
+    for core, (across, within) in enumerate(((prev, nxt), (nxt, prev))):
+        field[core, :96, :192] = np.concatenate([own[:96, OWN_YZ], within[:96, HALO_YZ]], 1)
+        field[core, 96:, :112] = np.concatenate([own[96:, OWN_X], within[96:, HALO_X]], 1)
+        field[core, :, 256:352] = across
         assert not own[:96, OWN_X].any() and not own[96:, OWN_YZ].any()
-        assert not any(h[:96, :32].any() or h[96:, 48:].any() for h in halo)
+        assert not within[:96, :32].any() and not within[96:, 48:].any()
     return [m.astype(jnp.bfloat16) for m in (send, field, line_matrix())]
 
 
 PAIRS = TILES // 2
-TURN = 122
+TURN = 126
 GROUP = 8
 HBM = pl.BlockSpec(memory_space=pltpu.HBM)
 VMEM = pl.BlockSpec(memory_space=pltpu.VMEM)
@@ -141,7 +142,7 @@
 
 
 def pack(*arrays):
-    out = [(96, NX), (192, NX), (192, 192), (192, 256), (256, 256)]
+    out = [(96, NX), (192, NX), (192, 192), (192, 384), (256, 256)]
     return pl.pallas_call(
         pack_kernel,
         out_shape=[jax.ShapeDtypeStruct(shape, jnp.bfloat16) for shape in out],
@@ -199,30 +200,32 @@
                 out_ref[row : row + 8, :] = value
 
 
-def zy_fields(w_ref, x_ref, a_ref, b_ref, high_ref, low_ref, cols):
-    half = slice(cols.start % (NX // 2), cols.start % (NX // 2) + cols.stop - cols.start)
-    yz = jnp.concatenate([x_ref[OWN_YZ, cols], a_ref[HALO_YZ, cols], b_ref[HALO_YZ, half]], axis=0)
-    x = jnp.concatenate([x_ref[OWN_X, cols], a_ref[HALO_X, cols], b_ref[HALO_X, half]], axis=0)
-    out = jnp.concatenate(
-        [
-            jnp.dot(w_ref[:96, :], yz, preferred_element_type=jnp.float32),
-            jnp.dot(w_ref[96:, :160], x, preferred_element_type=jnp.float32),
-        ],
-        axis=0,
-    )
-    high = out.astype(jnp.bfloat16)
-    high_ref[:, cols] = high
-    low_ref[:, cols] = (out - high.astype(jnp.float32)).astype(jnp.bfloat16)
-
-
-def first_image_kernel(w_ref, l_ref, x_ref, a_ref, b0_ref, b1_ref, send_ref, high_ref, low_ref):
+def own_fields_kernel(w_ref, x_ref, b0_ref, b1_ref, part_ref):
+    for n in range(0, NX, 512):
+        cols, b_ref = slice(n, n + 512), (b0_ref, b1_ref)[n // (NX // 2)]
+        half = slice(n % (NX // 2), n % (NX // 2) + 512)
+        yz = jnp.concatenate([x_ref[OWN_YZ, cols], b_ref[HALO_YZ, half]], axis=0)
+        x = jnp.concatenate([x_ref[OWN_X, cols], b_ref[HALO_X, half]], axis=0)
+        part_ref[:96, cols] = jnp.dot(w_ref[:96, :192], yz, preferred_element_type=jnp.float32)
+        part_ref[96:, cols] = jnp.dot(w_ref[96:, :112], x, preferred_element_type=jnp.float32)
+
+
+def own_fields(*arrays):
+    return image_call(own_fields_kernel, "own_fields", [jax.ShapeDtypeStruct((192, NX), jnp.float32)], *arrays)[0]
+
+
+def first_image_kernel(w_ref, l_ref, part_ref, a_ref, send_ref, high_ref, low_ref):
     core = core_index()
     for parity in range(2):
 
         @pl.when(core == 1 - parity)
         def _(parity=parity):
             for n in range(0, NX, 512):
-                zy_fields(w_ref, x_ref, a_ref, (b0_ref, b1_ref)[n // (NX // 2)], high_ref, low_ref, slice(n, n + 512))
+                cols = slice(n, n + 512)
+                out = part_ref[:, cols] + jnp.dot(w_ref[:, 256:352], a_ref[:, cols], preferred_element_type=jnp.float32)
+                high = out.astype(jnp.bfloat16)
+                high_ref[:, cols] = high
+                low_ref[:, cols] = (out - high.astype(jnp.float32)).astype(jnp.bfloat16)
             line_image(l_ref, high_ref, low_ref, parity, send_ref)
 
 
@@ -331,7 +334,8 @@
         to_chip, x, send_w, field_w, line_w = pack(*map(in_hbm, weights), x)
         from_chip = lax.ppermute(to_chip, "slab", across)
         from_core = [lax.ppermute(part, "slab", within) for part in pack_core(send_w, x)]
-        send, high, low = first_image(field_w, line_w, x, from_chip, *from_core)
+        part = own_fields(field_w, x, *from_core)
+        send, high, low = first_image(field_w, line_w, part, from_chip)
         other = lax.ppermute(send, "slab", within)
         keep = second_image(line_w, high, low)
         merged = merge(keep, other).reshape(128, 4, 128)

time: 46.8 us -> 46.5 us (level); the launches traced: 46.7 us -> 45.9 us
  starting transfers between devices: 19.1 us -> 18.4 us
  blocking collectives: 19.9 us -> 19.2 us
  Pallas kernels: 5.75 us -> 6.28 us
    all_to_all x1, blocking collectives: 19.9 us -> 19.2 us  [per_device(): lax.all_to_all(merged, 'slab', 0, 0, axis_index_groups=same_core, tiled=T...]
    ppermute x1, starting transfers between devices: 7.35 us -> 6.72 us  [per_device(): other = lax.ppermute(send, 'slab', within)]
    pallas_call x3 -> x4, Pallas kernels: 3.06 us -> 3.58 us  [image_call(): pl.pallas_call(kernel, out_shape=outs, in_specs=[VMEM] * len(arrays), out...]
  transfers between devices with their start and end apart: 4 -> 4, of which waited for: 3 -> 3; matrix products, arithmetic and copies ran while one was open for 0% -> 0% of each run, Pallas kernels for 3% -> 4%
where the time goes in v5:
time: 46.5 us; the launch traced here: 45.9 us
  blocking collectives  19.2 us (41%)
  starting transfers between devices  18.4 us (40%)
  Pallas kernels  6.28 us (14%)
  waiting for transfers between devices  1.96 us (4%)
    all_to_all x1, blocking collectives, per_device(): lax.all_to_all(merged, 'slab', 0, 0, axis_index_groups=same_core, tiled=T...  19.2 us
    ppermute x2, starting transfers between devices, per_device(): lax.ppermute(part, 'slab', within)  8.94 us
    ppermute x1, starting transfers between devices, per_device(): other = lax.ppermute(send, 'slab', within)  6.72 us
    pallas_call x4, Pallas kernels, image_call(): pl.pallas_call(kernel, out_shape=outs, in_specs=[VMEM] * len(arrays), out...  3.58 us
    ppermute x1, starting transfers between devices, per_device(): from_chip = lax.ppermute(to_chip, 'slab', across)  2.77 us
    ppermute x2, waiting for transfers between devices, per_device(): lax.ppermute(part, 'slab', within)  1.81 us
    pallas_call x1, Pallas kernels, pack(): pl.pallas_call(pack_kernel, out_shape=[jax.ShapeDtypeStruct(shape, jnp.bf...  1.78 us
  transfers between devices with their start and end apart: 4, of which 3 were waited for; matrix products, arithmetic and copies ran while one was open for 0% of the time, Pallas kernels for 4%

profile of v5, /device:TPU:1, one launch (start us, length us, event | category | flops | bytes accessed | tf_op | source)
XLA Modules:
  0.0 45.9 jit_solution(8791516940968955245)
XLA Ops:
  0.0 1.8 %pack_halo.1 = (bf16[96,4096]{1,0:T(8,128)(2,1)S(1)}, bf16[192,4096]{1,0:T(8,128)(2,1)S(1)}, bf16[192,192]{1,0:T(8,128)(2,1)S(1)}, bf16[192,384]{1,0:T(8,128)(2,1)S(1)}, bf16[256,256]{1,0:T(8,128)(2,1)S(1)}) custom-call(bf16[2,192,192]{2,1,0:T(8,128)(2,1)} %constant.6.clone.w_ref, bf16[2,192,384]{2,1,0:T(8,128)(2,1)} %constant.7.clone.f_ref, ...), custom_call_target="tpu_custom_call" | custom-call | tf_op jit(solution)/shard_map/pack_halo/pallas_call | solution.py:146
  1.8 2.8 %collective-permute-start.2 = (bf16[96,4096]{1,0:T(8,128)(2,1)S(1)}, bf16[96,4096]{1,0:T(8,128)(2,1)S(1)}, u32[]{:S(2)}, u32[]{:S(2)}) collective-permute-start(bf16[96,4096]{1,0:T(8,128)(2,1)S(1)} %get-tuple-element.21), channel_id=1, source_target_pairs={{0,255},{1,2},{2,1},{3,4},{4,3},{5,6},{6,5},{7,8},{8,7},{9,10},{10... | collective-permute-start | bytes 2359304 | tf_op jit(solution)/shard_map/ppermute | solution.py:335
  4.6 0.4 pack_core.1
  4.9 8.8 %collective-permute-start = (bf16[96,2048]{1,0:T(8,128)(2,1)S(1)}, bf16[96,2048]{1,0:T(8,128)(2,1)S(1)}, u32[]{:S(2)}, u32[]{:S(2)}) collective-permute-start(bf16[96,2048]{1,0:T(8,128)(2,1)S(1)} %get-tuple-element.19), channel_id=1, source_target_pairs={{0,1},{1,0},{2,3},{3,2},{4,5},{5,4},{6,7},{7,6},{8,9},{9,8},{10,11... | collective-permute-start | bytes 1179656 | tf_op jit(solution)/shard_map/ppermute | solution.py:336
  13.8 0.1 collective-permute-start.1
  13.9 1.2 %collective-permute-done.b0_ref = bf16[96,2048]{1,0:T(8,128)(2,1)S(1)} collective-permute-done((bf16[96,2048]{1,0:T(8,128)(2,1)S(1)}, bf16[96,2048]{1,0:T(8,128)(2,1)S(1)}, u32[]{:S(2)}, u32[]{:S(2)}) %collective-permute-start) | collective-permute-done | bytes 393248 | tf_op jit(solution)/shard_map/ppermute | solution.py:336
  15.1 0.6 %collective-permute-done.1.b1_ref = bf16[96,2048]{1,0:T(8,128)(2,1)S(1)} collective-permute-done((bf16[96,2048]{1,0:T(8,128)(2,1)S(1)}, bf16[96,2048]{1,0:T(8,128)(2,1)S(1)}, u32[]{:S(2)}, u32[]{:S(2)}) %collective-permute-start.1) | collective-permute-done | bytes 393248 | tf_op jit(solution)/shard_map/ppermute | solution.py:336
  15.7 0.6 %own_fields.1.part_ref = f32[192,4096]{1,0:T(8,128)S(1)} custom-call(bf16[192,384]{1,0:T(8,128)(2,1)S(1)} %get-tuple-element.16.w_ref, bf16[192,4096]{1,0:T(8,128)(2,1)S(1)} %get-tuple-element.17.x_ref, bf16[96,2048]{1,0:T(8,128)(2,1)S(1)} %collective-permute-done.b0_ref, bf16[96,2048]{1,0:T(8,128)(2,1)S(1)} %collective-permute-done.1.b1_ref), custom_call_target="tpu_custom_call" | custom-call | flops 1610612736 | bytes 1048576 | tf_op jit(solution)/shard_map/own_fields/pallas_call | solution.py:242
  16.3 0.0 collective-permute-done.2.a_ref
  16.3 1.6 %send_image.1 = (f32[512,128]{1,0:T(8,128)S(1)}, bf16[192,4096]{1,0:T(8,128)(2,1)S(1)}, bf16[192,4096]{1,0:T(8,128)(2,1)S(1)}) custom-call(bf16[192,384]{1,0:T(8,128)(2,1)S(1)} %get-tuple-element.16.w_ref, bf16[256,256]{1,0:T(8,128)(2,1)S(1)} %get-tuple-element.15.l_ref, f32[192,4096]{1,0:T(8,128)S(1)} %own_fields.1.part_ref, ...), custom_call_target="tpu_custom_call" | custom-call | flops 1610612736 | bytes 1048576 | tf_op jit(solution)/shard_map/send_image/pallas_call | solution.py:242
  17.9 6.7 %collective-permute-start.3 = (f32[512,128]{1,0:T(8,128)S(1)}, f32[512,128]{1,0:T(8,128)S(1)}, u32[]{:S(2)}, u32[]{:S(2)}) collective-permute-start(f32[512,128]{1,0:T(8,128)S(1)} %get-tuple-element.24), channel_id=1, source_target_pairs={{0,1},{1,0},{2,3},{3,2},{4,5},{5,4},{6,7},{7,6},{8,9},{9,8},{10,11... | collective-permute-start | bytes 786440 | tf_op jit(solution)/shard_map/ppermute | solution.py:339
  24.6 1.0 %keep_image.1.own_ref = f32[512,128]{1,0:T(8,128)S(1)} custom-call(bf16[256,256]{1,0:T(8,128)(2,1)S(1)} %get-tuple-element.15.l_ref, bf16[192,4096]{1,0:T(8,128)(2,1)S(1)} %get-tuple-element.22.high_ref, bf16[192,4096]{1,0:T(8,128)(2,1)S(1)} %get-tuple-element.23.low_ref), custom_call_target="tpu_custom_call" | custom-call | flops 1610612736 | bytes 1048576 | tf_op jit(solution)/shard_map/keep_image/pallas_call | solution.py:242
  25.7 0.1 collective-permute-done.3.other_ref
  25.8 0.2 merge_cores.1
  26.0 19.2 %all_to_all.5 = f32[128,4,128]{2,1,0:T(4,128)S(1)} all-to-all(f32[128,4,128]{2,1,0:T(4,128)S(1)} %bitcast.3), channel_id=1, replica_groups={{252,254,0,2,4,6,8,10,12,14,16,18,20,22,24,26,28,30,32,34,36,38,40,42,4..., dimensions={0} | all-to-all | bytes 524288 | tf_op jit(solution)/shard_map/all_to_all | solution.py:342
  45.2 0.7 %composite_chips.1 = f32[4,128]{1,0:T(4,128)} custom-call(f32[512,128]{1,0:T(8,128)S(1)} %bitcast.4), custom_call_target="tpu_custom_call" | custom-call | tf_op jit(solution)/shard_map/composite_chips/pallas_call | solution.py:315
Async XLA Ops:
  1.8 14.5 %collective-permute-start.2 = (bf16[96,4096]{1,0:T(8,128)(2,1)S(1)}, bf16[96,4096]{1,0:T(8,128)(2,1)S(1)}, u32[]{:S(2)}, u32[]{:S(2)}) collective-permute-start(bf16[96,4096]{1,0:T(8,128)(2,1)S(1)} %get-tuple-element.21), channel_id=1, source_target_pairs={{0,255},{1,2},{2,1},{3,4},{4,3},{5,6},{6,5},{7,8},{8,7},{9,10},{10... | collective-permute-start | bytes 2359304 | tf_op jit(solution)/shard_map/ppermute | solution.py:335
  4.9 10.2 %collective-permute-start = (bf16[96,2048]{1,0:T(8,128)(2,1)S(1)}, bf16[96,2048]{1,0:T(8,128)(2,1)S(1)}, u32[]{:S(2)}, u32[]{:S(2)}) collective-permute-start(bf16[96,2048]{1,0:T(8,128)(2,1)S(1)} %get-tuple-element.19), channel_id=1, source_target_pairs={{0,1},{1,0},{2,3},{3,2},{4,5},{5,4},{6,7},{7,6},{8,9},{9,8},{10,11... | collective-permute-start | bytes 1179656 | tf_op jit(solution)/shard_map/ppermute | solution.py:336
  13.8 1.9 %collective-permute-start.1 = (bf16[96,2048]{1,0:T(8,128)(2,1)S(1)}, bf16[96,2048]{1,0:T(8,128)(2,1)S(1)}, u32[]{:S(2)}, u32[]{:S(2)}) collective-permute-start(bf16[96,2048]{1,0:T(8,128)(2,1)S(1)} %get-tuple-element.20), channel_id=1, source_target_pairs={{0,1},{1,0},{2,3},{3,2},{4,5},{5,4},{6,7},{7,6},{8,9},{9,8},{10,11... | collective-permute-start | bytes 1179656 | tf_op jit(solution)/shard_map/ppermute | solution.py:336
  17.9 7.9 %collective-permute-start.3 = (f32[512,128]{1,0:T(8,128)S(1)}, f32[512,128]{1,0:T(8,128)S(1)}, u32[]{:S(2)}, u32[]{:S(2)}) collective-permute-start(f32[512,128]{1,0:T(8,128)S(1)} %get-tuple-element.24), channel_id=1, source_target_pairs={{0,1},{1,0},{2,3},{3,2},{4,5},{5,4},{6,7},{7,6},{8,9},{9,8},{10,11... | collective-permute-start | bytes 786440 | tf_op jit(solution)/shard_map/ppermute | solution.py:339
